TPU v7x, 32 devices: a whole 2x2x4 slice. The times are simulated.
32 devices in a mesh: groups: 2 (over x), cross: 8 (over z, y), node: 2 (over core).
Axes of the slice: x: 2, y: 2, z: 4, core: 2. Of those that a mesh axis runs over, the one named last changes fastest.
Arguments:
- tokens: bfloat16 [4096, 2560], P(('groups', 'cross', 'node')), parts along dimension 0, may hold values from -0.59765625 to 0.59765625
- grad_out: bfloat16 [4096, 2560], P(('groups', 'cross', 'node')), parts along dimension 0, may hold values from -6 to 6
- expert_ids: int32 [4096, 1], P(('groups', 'cross', 'node')), parts along dimension 0, may hold values from 0 to 1; in each aligned block of 128 rows (0 to 127, 128 to 255, ...) at most 72 rows name the same one
- routed_pre: bfloat16 [2, 4608, 4096], P(None, ('groups', 'node'), 'cross'), parts along dimension 1, may hold values from -6 to 6
- shared_pre: bfloat16 [2, 4608, 4096], P(None, ('groups', 'node'), 'cross'), parts along dimension 1, may hold values from -6 to 6
- w_gate: bfloat16 [2, 2560, 4096], P('node', None, 'cross'), may hold values from -0.125 to 0.125
- w_up: bfloat16 [2, 2560, 4096], P('node', None, 'cross'), may hold values from -0.125 to 0.125
- w_down: bfloat16 [2, 4096, 2560], P('node', 'cross'), may hold values from -0.09375 to 0.09375
- s_gate: bfloat16 [2560, 4096], P(None, 'cross'), may hold values from -0.125 to 0.125
- s_up: bfloat16 [2560, 4096], P(None, 'cross'), may hold values from -0.125 to 0.125
- s_down: bfloat16 [4096, 2560], P('cross'), may hold values from -0.09375 to 0.09375
Outputs:
- grad_tokens: bfloat16 [4096, 2560], P(('groups', 'cross', 'node')), parts along dimension 0
- grad_shared_gate: float32 [5120, 4096], P(('groups', 'node'), 'cross'), parts along dimension 0
- grad_shared_up: float32 [5120, 4096], P(('groups', 'node'), 'cross'), parts along dimension 0
- grad_shared_down: float32 [8192, 2560], P(('groups', 'cross'), 'node'), parts along dimension 0
There are 2 independent parts, one for each index of `groups`. A program takes and returns all parts, laid end to end along the dimension named above; an argument that names none is the same for every part. Nothing has to cross between parts.
Inputs may be any that keep to these rules, and one draw needn't show every extreme that they name: `expert_ids`: within the tokens of one device (aligned blocks of 128 rows) no expert is named more than 72 times, and in every draw some block names some expert exactly 72 times. Rows of routed_pre and shared_pre whose slot holds no token are read by no output.
All inputs are finite; a program needn't handle non-finite values.
Results may differ from a plain program's by a relative error of at most 0.012.
Values may be sent and summed in bfloat16 or wider, within the bound.
A program may use at most 256 MiB of HBM per device.

v0:
```python
import jax
import jax.numpy as jnp
from jax import lax
from jax.sharding import PartitionSpec as P

CAP = 72


def silu_parts(pre_gate, pre_up, grad_hidden):
    sigma = jax.nn.sigmoid(pre_gate)
    active = pre_gate * sigma
    d_gate = grad_hidden * pre_up * sigma * (1.0 + pre_gate * (1.0 - sigma))
    d_up = grad_hidden * active
    return (d_gate, d_up, active * pre_up)


def right_t(left, right):
    return lax.dot_general(
        left, right, (((1,), (1,)), ((), ())), preferred_element_type=jnp.float32
    )


def left_t(left, right):
    return lax.dot_general(
        left, right, (((0,), (0,)), ((), ())), preferred_element_type=jnp.float32
    )


def body(
    tokens, grad_out, expert_ids, routed_pre, shared_pre, w_gate, w_up, w_down, s_gate, s_up, s_down
):
    experts = lax.axis_size("node")
    cross_count = lax.axis_size("cross")
    width = tokens.shape[1]
    ids = expert_ids[:, 0]
    onehot = (ids[:, None] == jnp.arange(experts, dtype=jnp.int32)[None, :]).astype(jnp.int32)
    ranks = jnp.cumsum(onehot, axis=0) - 1
    dest = ids * CAP + jnp.sum(ranks * onehot, axis=1)
    dy_send = jnp.zeros((experts * CAP, width), jnp.bfloat16).at[dest].set(grad_out)
    x_send = jnp.zeros((experts * CAP, width), jnp.bfloat16).at[dest].set(tokens)
    dy_wide, x_wide = (
        lax.all_gather(dy_send.reshape(1, experts, CAP, width), "cross", axis=0, tiled=True),
        lax.all_gather(x_send.reshape(1, experts, CAP, width), "cross", axis=0, tiled=True),
    )
    dy_all, x_all = (
        lax.all_to_all(dy_wide, "node", split_axis=1, concat_axis=1, tiled=True),
        lax.all_to_all(x_wide, "node", split_axis=1, concat_axis=1, tiled=True),
    )
    dy_rows = dy_all.reshape(-1, width)
    x_rows = x_all.reshape(-1, width)
    d_gate, d_up, unused = silu_parts(
        routed_pre[0].astype(jnp.float32),
        routed_pre[1].astype(jnp.float32),
        right_t(dy_rows, w_down[0]),
    )
    sh_gate, sh_up, shared_act = silu_parts(
        shared_pre[0].astype(jnp.float32),
        shared_pre[1].astype(jnp.float32),
        right_t(dy_rows, s_down),
    )
    d_gate = d_gate.astype(jnp.bfloat16)
    d_up = d_up.astype(jnp.bfloat16)
    sh_gate = sh_gate.astype(jnp.bfloat16)
    sh_up = sh_up.astype(jnp.bfloat16)
    shared_act = shared_act.astype(jnp.bfloat16)
    partial_in = (
        right_t(d_gate, w_gate[0])
        + right_t(d_up, w_up[0])
        + right_t(sh_gate, s_gate)
        + right_t(sh_up, s_up)
    )
    partial_in = partial_in.astype(jnp.bfloat16)
    summed = lax.psum_scatter(
        partial_in.reshape(cross_count, experts * CAP, width),
        "cross",
        scatter_dimension=0,
        tiled=True,
    ).astype(jnp.float32)
    returned = summed.reshape(experts, CAP, width).astype(jnp.bfloat16)
    returned = lax.all_to_all(returned, "node", split_axis=0, concat_axis=0, tiled=True)
    grad_tokens = returned.reshape(experts * CAP, width)[dest]
    grad_gate = left_t(x_rows, sh_gate)
    grad_up = left_t(x_rows, sh_up)
    grad_down = left_t(shared_act, dy_rows)
    grad_gate, grad_up, grad_down = (
        lax.psum(grad_gate.astype(jnp.bfloat16), "node").astype(jnp.float32),
        lax.psum(grad_up.astype(jnp.bfloat16), "node").astype(jnp.float32),
        lax.psum(grad_down.astype(jnp.bfloat16), "node").astype(jnp.float32),
    )
    share = width // experts
    offset = lax.axis_index("node") * share
    grad_gate = lax.dynamic_slice_in_dim(grad_gate, offset, share, 0)
    grad_up = lax.dynamic_slice_in_dim(grad_up, offset, share, 0)
    grad_down = lax.dynamic_slice_in_dim(grad_down, offset, share, 1)
    return (grad_tokens, grad_gate, grad_up, grad_down)


def solution(mesh):
    in_specs = (
        P(("groups", "cross", "node"), None),
        P(("groups", "cross", "node"), None),
        P(("groups", "cross", "node"), None),
        P(None, ("groups", "node"), "cross"),
        P(None, ("groups", "node"), "cross"),
        P("node", None, "cross"),
        P("node", None, "cross"),
        P("node", "cross", None),
        P(None, "cross"),
        P(None, "cross"),
        P("cross", None),
    )
    out_specs = (
        P(("groups", "cross", "node"), None),
        P(("groups", "node"), "cross"),
        P(("groups", "node"), "cross"),
        P(("groups", "cross"), "node"),
    )
    return jax.shard_map(body, mesh=mesh, in_specs=in_specs, out_specs=out_specs, check_vma=False)
```

profile of v0, /device:TPU:0, one launch (start us, length us, event | category | flops | bytes accessed | tf_op | source)
XLA Modules:
  0.0 394.7 jit_solution(945681576662736524)
XLA Ops:
  7.2 0.9 fusion.50
  9.8 3.0 scatter_custom_fusion
  12.8 3.0 scatter_custom_fusion.1
  15.9 94.0 %all-gather.3.cloned.1.call-done = bf16[8,2,72,2560]{3,2,1,0:T(8,128)(2,1)} async-done(((bf16[1,2,72,2560]{3,2,1,0:T(8,128)(2,1)}), bf16[8,2,72,2560]{3,2,1,0:T(8,128)(2,1)}) %all-gather.3.cloned.1.call-update) | async-done | bytes 5898256 | tf_op jit(solution)/shard_map/all_gather | solution.py:42
  109.9 3.1 copy.17
  113.0 8.5 %all_to_all.15 = bf16[8,2,72,2560]{3,2,0,1:T(8,128)(2,1)S(1)} all-to-all(bf16[8,2,72,2560]{3,2,0,1:T(8,128)(2,1)S(1)} %copy.17), channel_id=1, replica_groups=mesh['groups'=2,'cross'=8,'node'=2] {'node'}, dimensions={1} | all-to-all | bytes 11796480 | tf_op jit(solution)/shard_map/all_to_all | solution.py:46
  122.1 1.3 copy-done.10
  123.4 5.3 %convolution_convert_fusion = bf16[512,2560]{1,0:T(8,128)(2,1)} fusion(bf16[1152,2560]{1,0:T(8,128)(2,1)S(1)} %bitcast.92, bf16[2,1152,512]{2,1,0:T(8,128)(2,1)S(1)} %copy-done.10), kind=kOutput, calls=%fused_computation.7 | convolution fusion | flops 3025928192 | bytes 10878976 | tf_op jit(solution)/shard_map/dot_general | solution.py:24
  128.7 5.9 %fusion.12 = (bf16[1152,512]{1,0:T(8,128)(2,1)}, f32[1152,512]{1,0:T(8,128)}) fusion(bf16[2,1152,512]{2,1,0:T(8,128)(2,1)S(1)} %copy-done.10, bf16[1152,2560]{1,0:T(8,128)(2,1)S(1)} %bitcast.93, bf16[512,2560]{1,0:T(8,128)(2,1)S(1)} %copy-done.8), kind=kOutput, calls=%fused_computation.29 | convolution fusion | flops 3026976768 | bytes 14417920 | tf_op jit(solution)/shard_map/dot_general | solution.py:18
  134.6 70.5 %all-gather.5.cloned.1.call-done = bf16[8,2,72,2560]{3,2,1,0:T(8,128)(2,1)} async-done(((bf16[1,2,72,2560]{3,2,1,0:T(8,128)(2,1)}), bf16[8,2,72,2560]{3,2,1,0:T(8,128)(2,1)}) %all-gather.5.cloned.1.call-update) | async-done | bytes 5898256 | tf_op jit(solution)/shard_map/all_gather | solution.py:43
  205.1 3.1 copy.19
  208.2 8.5 %all_to_all.16 = bf16[8,2,72,2560]{3,2,0,1:T(8,128)(2,1)S(1)} all-to-all(bf16[8,2,72,2560]{3,2,0,1:T(8,128)(2,1)S(1)} %copy.19), channel_id=1, replica_groups=mesh['groups'=2,'cross'=8,'node'=2] {'node'}, dimensions={1} | all-to-all | bytes 11796480 | tf_op jit(solution)/shard_map/all_to_all | solution.py:47
  218.0 4.9 %convolution_convert_fusion.2 = bf16[2560,512]{1,0:T(8,128)(2,1)} fusion(bf16[1152,2560]{1,0:T(8,128)(2,1)S(1)} %bitcast.95, bf16[1152,512]{1,0:T(8,128)(2,1)S(1)} %copy-done.3), kind=kOutput, calls=%fused_computation.9 | convolution fusion | flops 3021209600 | bytes 9699328 | tf_op jit(solution)/shard_map/dot_general | solution.py:24
  222.9 5.2 %convolution_convert_fusion.1 = bf16[2560,512]{1,0:T(8,128)(2,1)} fusion(bf16[1152,2560]{1,0:T(8,128)(2,1)S(1)} %bitcast.96, f32[1152,512]{1,0:T(8,128)S(1)} %copy-done.12, bf16[2,1152,512]{2,1,0:T(8,128)(2,1)S(1)} %copy-done.11), kind=kOutput, calls=%fused_computation.8 | convolution fusion | flops 3025338368 | bytes 12058624 | tf_op jit(solution)/shard_map/dot_general | solution.py:24
  228.1 6.2 %fusion.7 = f32[1152,512]{1,0:T(8,128)S(1)} fusion(bf16[1152,2560]{1,0:T(8,128)(2,1)} %bitcast.94, bf16[1,512,2560]{2,1,0:T(8,128)(2,1)} %param.18), kind=kOutput, calls=%fused_computation.24 | convolution fusion | flops 3019898880 | bytes 10878976 | tf_op jit(solution)/shard_map/dot_general | solution.py:18
  234.4 7.7 %fusion.5 = f32[1152,2560]{1,0:T(8,128)} fusion(bf16[1,2560,512]{2,1,0:T(8,128)(2,1)S(1)} %copy-done, f32[1152,512]{1,0:T(8,128)S(1)} %fusion.7, bf16[2,1152,512]{2,1,0:T(8,128)(2,1)S(1)} %copy-done.6), kind=kOutput, calls=%fused_computation.22 | convolution fusion | flops 3026976768 | bytes 19136512 | tf_op jit(solution)/shard_map/dot_general | solution.py:18
  242.1 7.6 %convolution_add_fusion.2 = f32[1152,2560]{1,0:T(8,128)S(1)} fusion(f32[1152,2560]{1,0:T(8,128)} %fusion.5, bf16[1,2560,512]{2,1,0:T(8,128)(2,1)S(1)} %copy-done.5, f32[1152,512]{1,0:T(8,128)S(1)} %fusion.7, bf16[2,1152,512]{2,1,0:T(8,128)(2,1)} %param.14), kind=kOutput, calls=%fused_computation.5 | convolution fusion | flops 3026976768 | bytes 29753344 | tf_op jit(solution)/shard_map/dot_general | solution.py:18
  249.7 9.9 %convolution_add_fusion.1 = f32[1152,2560]{1,0:T(8,128)} fusion(f32[1152,2560]{1,0:T(8,128)S(1)} %convolution_add_fusion.2, bf16[1152,512]{1,0:T(8,128)(2,1)S(1)} %copy-done.4, bf16[2560,512]{1,0:T(8,128)(2,1)} %param.19), kind=kOutput, calls=%fused_computation.4 | convolution fusion | flops 3022848000 | bytes 27394048 | tf_op jit(solution)/shard_map/dot_general | solution.py:18
  259.6 9.7 %fusion = bf16[1152,2560]{1,0:T(8,128)(2,1)} fusion(f32[1152,2560]{1,0:T(8,128)} %convolution_add_fusion.1, bf16[2560,512]{1,0:T(8,128)(2,1)S(1)} %copy-done.9, f32[1152,512]{1,0:T(8,128)} %get-tuple-element.8, bf16[2,1152,512]{2,1,0:T(8,128)(2,1)} %param.15), kind=kOutput, calls=%fused_computation.6 | convolution fusion | flops 3029925888 | bytes 23855104 | tf_op jit(solution)/shard_map/dot_general | solution.py:18
  269.4 3.1 dynamic-slice_convert_fusion
  272.6 4.4 %dynamic-slice_convert_fusion.1 = (f32[1280,512]{1,0:T(8,128)}, f32[1280,512]{1,0:T(8,128)}) fusion(bf16[2560,512]{1,0:T(8,128)(2,1)} %get-tuple-element.5, s32[]{:T(128)S(6)} %select_n.12, bf16[2560,512]{1,0:T(8,128)(2,1)S(1)} %copy-done.7), kind=kLoop, calls=%fused_computation.51 | loop fusion | flops 1310720 | bytes 7864324 | tf_op jit(solution)/shard_map/convert_element_type | solution.py:87
  277.0 103.9 %reduce-scatter.2.cloned.1.call-done = bf16[1,144,2560]{2,1,0:T(8,128)(2,1)} async-done(((bf16[8,144,2560]{2,1,0:T(8,128)(2,1)}), bf16[1,144,2560]{2,1,0:T(8,128)(2,1)}) %reduce-scatter.2.cloned.1.call-update) | async-done | bytes 737296 | tf_op jit(solution)/shard_map/reduce_scatter | solution.py:73
  380.9 5.4 %all_to_all.17 = bf16[2,72,2560]{2,1,0:T(8,128)(2,1)S(1)} all-to-all(bf16[2,72,2560]{2,1,0:T(8,128)(2,1)} %bitcast.99), channel_id=1, replica_groups=mesh['groups'=2,'cross'=8,'node'=2] {'node'}, dimensions={0} | all-to-all | bytes 1474560 | tf_op jit(solution)/shard_map/all_to_all | solution.py:80
  386.3 1.8 gather_fusion
  (40 shorter events, 3.8 us)
Async XLA Ops:
  7.2 227.2 %copy-start = (bf16[1,2560,512]{2,1,0:T(8,128)(2,1)S(1)}, bf16[1,2560,512]{2,1,0:T(8,128)(2,1)}, u32[]{:S(2)}) copy-start(bf16[1,2560,512]{2,1,0:T(8,128)(2,1)} %param.16) | copy-start | bytes 7864324
  7.2 102.7 %all-gather.3.cloned.1.call-start = ((), (), s32[]{:S(2)}) async-start(), calls=%async_computation.4 | async-start | bytes 6635520 | tf_op jit(solution)/shard_map/all_gather | solution.py:42
  12.8 192.3 %all-gather.5.cloned.1.call-start = ((), (), s32[]{:S(2)}) async-start(), calls=%async_computation.6 | async-start | bytes 6635520 | tf_op jit(solution)/shard_map/all_gather | solution.py:43
  15.8 253.6 %all-reduce.3.cloned.1.call-start = ((), (), s32[]{:S(2)}) async-start(), calls=%async_computation.7 | async-start | bytes 15728640 | tf_op jit(solution)/shard_map/psum | solution.py:86
  121.5 1.9 copy-start.10
  122.1 6.6 %copy-start.2 = (bf16[8,2,72,2560]{3,2,1,0:T(8,128)(2,1)}, bf16[8,2,72,2560]{3,2,1,0:T(8,128)(2,1)S(1)}, u32[]{:S(2)}) copy-start(bf16[8,2,72,2560]{3,2,1,0:T(8,128)(2,1)S(1)} %copy.18) | copy-start | bytes 17694724
  123.4 5.3 %copy-start.8 = (bf16[512,2560]{1,0:T(8,128)(2,1)S(1)}, bf16[512,2560]{1,0:T(8,128)(2,1)}, u32[]{:S(2)}) copy-start(bf16[512,2560]{1,0:T(8,128)(2,1)} %param.21) | copy-start | bytes 7864324
  216.7 1.3 copy-start.3
  218.0 4.9 %copy-start.11 = (bf16[2,1152,512]{2,1,0:T(8,128)(2,1)S(1)}, bf16[2,1152,512]{2,1,0:T(8,128)(2,1)}, u32[]{:S(2)}) copy-start(bf16[2,1152,512]{2,1,0:T(8,128)(2,1)} %param.15) | copy-start | bytes 7077892
  218.0 4.9 %copy-start.12 = (f32[1152,512]{1,0:T(8,128)S(1)}, f32[1152,512]{1,0:T(8,128)}, u32[]{:S(2)}) copy-start(f32[1152,512]{1,0:T(8,128)} %get-tuple-element.8) | copy-start | bytes 7077892
  228.1 152.8 %reduce-scatter.2.cloned.1.call-start = ((), (), s32[]{:S(2)}) async-start(), calls=%async_computation.5 | async-start | bytes 6635520 | tf_op jit(solution)/shard_map/reduce_scatter | solution.py:73
  228.1 6.3 %copy-start.6 = (bf16[2,1152,512]{2,1,0:T(8,128)(2,1)S(1)}, bf16[2,1152,512]{2,1,0:T(8,128)(2,1)}, u32[]{:S(2)}) copy-start(bf16[2,1152,512]{2,1,0:T(8,128)(2,1)} %param.14) | copy-start | bytes 7077892
  234.4 7.7 %copy-start.5 = (bf16[1,2560,512]{2,1,0:T(8,128)(2,1)S(1)}, bf16[1,2560,512]{2,1,0:T(8,128)(2,1)}, u32[]{:S(2)}) copy-start(bf16[1,2560,512]{2,1,0:T(8,128)(2,1)} %param.17) | copy-start | bytes 7864324
  242.1 7.6 %copy-start.4 = (bf16[1152,512]{1,0:T(8,128)(2,1)S(1)}, bf16[1152,512]{1,0:T(8,128)(2,1)}, u32[]{:S(2)}) copy-start(bf16[1152,512]{1,0:T(8,128)(2,1)} %get-tuple-element.7) | copy-start | bytes 3538948
  249.7 9.9 %copy-start.9 = (bf16[2560,512]{1,0:T(8,128)(2,1)S(1)}, bf16[2560,512]{1,0:T(8,128)(2,1)}, u32[]{:S(2)}) copy-start(bf16[2560,512]{1,0:T(8,128)(2,1)} %param.20) | copy-start | bytes 7864324
  269.4 3.2 copy-start.7
  386.3 1.8 copy-start.1
Sparse Core Ops, SparseCore 0:
  12.9 96.9 all-gather.2
  112.6 92.4 all-gather.4
  228.2 33.4 all-reduce.2
  269.5 111.3 reduce-scatter.1
where the time goes:
time: 395 us
  waiting for transfers between devices  269 us (68%)
  matrix products  62.4 us (16%)
  blocking collectives  22.4 us (6%)
  local copies, waits for them, and re-layouts  17.2 us (4%)
  between operations  13.9 us (4%)
  other arithmetic  10.1 us (3%)
    reduce_scatter x1, waiting for transfers between devices, body(): lax.psum_scatter(partial_in.reshape(cross_count, experts * CAP, width), '...  104 us
    all_gather x1, waiting for transfers between devices, body(): lax.all_gather(dy_send.reshape(1, experts, CAP, width), 'cross', axis=0,...  94 us
    all_gather x1, waiting for transfers between devices, body(): lax.all_gather(x_send.reshape(1, experts, CAP, width), 'cross', axis=0, t...  70.5 us
    dot_general x6, matrix products, right_t(): lax.dot_general(left, right, (((1,), (1,)), ((), ())), preferred_element_...  47 us
    dot_general x3, matrix products, left_t(): lax.dot_general(left, right, (((0,), (0,)), ((), ())), preferred_element_...  15.4 us
    all_to_all x1, blocking collectives, body(): lax.all_to_all(x_wide, 'node', split_axis=1, concat_axis=1, tiled=True)  8.47 us
    all_to_all x1, blocking collectives, body(): lax.all_to_all(dy_wide, 'node', split_axis=1, concat_axis=1, tiled=True)  8.47 us
  transfers between devices with their start and end apart: 4, of which 3 were waited for; matrix products, arithmetic and copies ran while one was open for 17% of the time, Pallas kernels for 0%

commit v1 on v0

v1 whole, which is shorter than its diff:
```python
import functools

import jax
import jax.numpy as jnp
from jax import lax
from jax.experimental import pallas as pl
from jax.experimental.pallas import tpu as pltpu
from jax.sharding import PartitionSpec as P

CAP = 72
MESH = pl.DeviceIdType.MESH
GATHER_PIECES = 2
REDUCE_PIECES = 3


def silu_parts(pre_gate, pre_up, grad_hidden):
    sigma = jax.nn.sigmoid(pre_gate)
    active = pre_gate * sigma
    d_gate = grad_hidden * pre_up * sigma * (1.0 + pre_gate * (1.0 - sigma))
    d_up = grad_hidden * active
    return (d_gate, d_up, active * pre_up)


def right_t(left, right):
    return lax.dot_general(
        left, right, (((1,), (1,)), ((), ())), preferred_element_type=jnp.float32
    )


def left_t(left, right):
    return lax.dot_general(
        left, right, (((0,), (0,)), ((), ())), preferred_element_type=jnp.float32
    )


def place(depth):
    cross = lax.axis_index("cross")
    return lax.div(cross, 2), lax.rem(cross, 2), lax.axis_index("node")


def greet(z, y, n, depth):
    barrier = pltpu.get_barrier_semaphore()

    def tell(zz, yy, nn):
        pl.semaphore_signal(
            barrier, inc=1, device_id={"cross": zz * 2 + yy, "node": nn}, device_id_type=MESH
        )

    tell(z, 1 - y, n)
    tell(z, y, 1 - n)

    @pl.when(z < depth - 1)
    def _():
        tell(z + 1, y, n)

    @pl.when(z > 0)
    def _():
        tell(z - 1, y, n)

    count = 2 + (z < depth - 1).astype(jnp.int32) + (z > 0).astype(jnp.int32)
    pl.semaphore_wait(barrier, count)


def gather_kernel(
    depth, dy, ids, x, dy_all, ids_all, xh,
    recv, recv_b, send_r, send_l, send_y, send_b, x_send, x_recv, local_sem,
):
    z, y, n = place(depth)
    rows = dy.shape[0] // GATHER_PIECES
    half = xh.shape[-1]
    pieces = GATHER_PIECES + 1
    greet(z, y, n, depth)

    def slot(c, core, h):
        if h < GATHER_PIECES:
            return dy_all.at[c, core, pl.ds(h * rows, rows)]
        return ids_all.at[c, core]

    def own(h):
        if h < GATHER_PIECES:
            return dy.at[pl.ds(h * rows, rows)]
        return ids

    def copy(src, c, h, send_sem, recv_sem, zz, yy, nn):
        return pltpu.make_async_remote_copy(
            src_ref=src,
            dst_ref=slot(c, n, h),
            send_sem=send_sem,
            recv_sem=recv_sem.at[c, h],
            device_id={"cross": zz * 2 + yy, "node": nn},
            device_id_type=MESH,
        )

    def right(src, zb, h):
        return copy(src, zb * 2 + y, h, send_r.at[zb, h], recv, z + 1, y, n)

    def left(src, zb, h):
        return copy(src, zb * 2 + y, h, send_l.at[zb, h], recv, z - 1, y, n)

    def across(src, zb, h):
        return copy(src, zb * 2 + y, h, send_y.at[zb, h], recv, z, 1 - y, n)

    def sibling(src, c, h):
        return copy(src, c, h, send_b.at[c, h], recv_b, z, y, 1 - n)

    def arrived(c, h):
        pltpu.make_async_remote_copy(
            src_ref=slot(c, n, h), dst_ref=slot(c, n, h), send_sem=send_b.at[c, h],
            recv_sem=recv.at[c, h], device_id={"cross": z * 2 + y, "node": 1 - n},
            device_id_type=MESH,
        ).wait_recv()

    def arrived_b(c, h):
        pltpu.make_async_remote_copy(
            src_ref=slot(c, 1 - n, h), dst_ref=slot(c, 1 - n, h), send_sem=send_b.at[c, h],
            recv_sem=recv_b.at[c, h], device_id={"cross": z * 2 + y, "node": 1 - n},
            device_id_type=MESH,
        ).wait_recv()

    def mine(src, zb, h, act):
        @pl.when((z < depth - 1) & (zb <= z))
        def _():
            act(right(src, zb, h))

        @pl.when((z > 0) & (zb >= z))
        def _():
            act(left(src, zb, h))

        act(across(src, zb, h))
        act(sibling(src, zb * 2 + y, h))

    def start(d):
        d.start()

    def done(d):
        d.wait_send()

    def walk(s, act):
        if s == 0:
            act(z)
        else:
            @pl.when(z - s >= 0)
            def _():
                act(z - s)

            @pl.when(z + s < depth)
            def _():
                act(z + s)

    order = [GATHER_PIECES] + list(range(GATHER_PIECES))
    for h in order:
        mine(own(h), z, h, start)
    keep = pl.multiple_of(n * half, 128)
    give = pl.multiple_of((1 - n) * half, 128)
    x_out = pltpu.make_async_remote_copy(
        src_ref=x.at[:, pl.ds(give, half)], dst_ref=xh.at[n], send_sem=x_send, recv_sem=x_recv,
        device_id={"cross": z * 2 + y, "node": 1 - n}, device_id_type=MESH,
    )
    x_out.start()
    locals_ = [
        pltpu.make_async_copy(dy, dy_all.at[z * 2 + y, n], local_sem.at[0]),
        pltpu.make_async_copy(ids, ids_all.at[z * 2 + y, n], local_sem.at[1]),
        pltpu.make_async_copy(x.at[:, pl.ds(keep, half)], xh.at[n], local_sem.at[2]),
    ]
    for d in locals_:
        d.start()

    def down(h):
        def act(zb):
            arrived(zb * 2 + y, h)
            mine(slot(zb * 2 + y, n, h), zb, h, start)
        return act

    def over(h):
        def act(zb):
            c = zb * 2 + 1 - y
            arrived(c, h)
            sibling(slot(c, n, h), c, h).start()
        return act

    for s in range(1, depth + 1):
        for h in order:
            if s < depth:
                walk(s, down(h))
            walk(s - 1, over(h))

    for d in locals_:
        d.wait()
    x_out.wait_send()
    pltpu.make_async_remote_copy(
        src_ref=xh.at[1 - n], dst_ref=xh.at[1 - n], send_sem=x_send, recv_sem=x_recv,
        device_id={"cross": z * 2 + y, "node": 1 - n}, device_id_type=MESH,
    ).wait_recv()
    for h in range(pieces):
        for zb in range(depth):
            mine(slot(zb * 2 + y, n, h), zb, h, done)
            c = zb * 2 + 1 - y
            sibling(slot(c, n, h), c, h).wait_send()
            arrived_b(zb * 2, h)
            arrived_b(zb * 2 + 1, h)


def gather(dy, ids, x, count):
    depth = count // 2
    rows, width = dy.shape
    pieces = GATHER_PIECES + 1
    dma = pltpu.SemaphoreType.DMA
    hbm = pl.BlockSpec(memory_space=pl.ANY)
    return pl.pallas_call(
        functools.partial(gather_kernel, depth),
        out_shape=(
            jax.ShapeDtypeStruct((count, 2, rows, width), dy.dtype),
            jax.ShapeDtypeStruct((count, 2) + ids.shape, ids.dtype),
            jax.ShapeDtypeStruct((2, rows, width // 2), x.dtype),
        ),
        in_specs=[hbm] * 3,
        out_specs=(hbm,) * 3,
        scratch_shapes=[
            dma((count, pieces)),
            dma((count, pieces)),
            dma((depth, pieces)),
            dma((depth, pieces)),
            dma((depth, pieces)),
            dma((count, pieces)),
            dma,
            dma,
            dma((3,)),
        ],
        compiler_params=pltpu.CompilerParams(collective_id=0, has_side_effects=True),
        name="gather_rows",
    )(dy, ids, x)


def reduce_kernel(
    depth, part, out, y_buf, r_buf, l_buf, held,
    y_send, y_recv, r_send, r_recv, l_send, l_recv, b_send, b_recv,
):
    z, y, n = place(depth)
    rows = part.shape[2] // REDUCE_PIECES
    greet(z, y, n, depth)

    def at(ref, d, h):
        return ref.at[d, pl.ds(h * rows, rows)]

    def copy(src, dst, send_sem, recv_sem, zz, yy, nn):
        return pltpu.make_async_remote_copy(
            src_ref=src, dst_ref=dst, send_sem=send_sem, recv_sem=recv_sem,
            device_id={"cross": zz * 2 + yy, "node": nn}, device_id_type=MESH,
        )

    def across(d, h):
        return copy(
            part.at[d, 1 - y, pl.ds(h * rows, rows)], at(y_buf, d, h),
            y_send.at[d, h], y_recv.at[d, h], z, 1 - y, n,
        )

    def right(d, h):
        return copy(
            at(held, d, h), at(r_buf, d, h), r_send.at[d, h], r_recv.at[d, h], z + 1, y, n
        )

    def left(d, h):
        return copy(
            at(held, d, h), at(l_buf, d, h), l_send.at[d, h], l_recv.at[d, h], z - 1, y, n
        )

    def sibling(h):
        return copy(
            at(out, n, h), at(out, n, h), b_send.at[h], b_recv.at[h], z, y, 1 - n
        )

    def walk(s, act):
        if s == 0:
            act(z)
        else:
            @pl.when(z + s < depth)
            def _():
                act(z + s)

            @pl.when(z - s >= 0)
            def _():
                act(z - s)

    def begin(s):
        for h in range(REDUCE_PIECES):
            walk(s, lambda d, h=h: across(d, h).start())

    def base(d, h):
        across(d, h).wait_recv()
        return part[d, y, pl.ds(h * rows, rows)].astype(jnp.float32) + y_buf[
            d, pl.ds(h * rows, rows)
        ].astype(jnp.float32)

    begin(depth - 1)
    for s in range(depth - 1, 0, -1):
        begin(s - 1)
        for h in range(REDUCE_PIECES):
            span = pl.ds(h * rows, rows)

            @pl.when(z + s < depth)
            def _():
                d = z + s
                value = base(d, h)
                if s == depth - 1:
                    held[d, span] = value.astype(held.dtype)
                else:
                    @pl.when(z == 0)
                    def _():
                        held[d, span] = value.astype(held.dtype)

                    @pl.when(z > 0)
                    def _():
                        right(d, h).wait_recv()
                        total = value + r_buf[d, span].astype(jnp.float32)
                        held[d, span] = total.astype(held.dtype)

                right(d, h).start()

            @pl.when(z - s >= 0)
            def _():
                d = z - s
                value = base(d, h)
                if s == depth - 1:
                    held[d, span] = value.astype(held.dtype)
                else:
                    @pl.when(z == depth - 1)
                    def _():
                        held[d, span] = value.astype(held.dtype)

                    @pl.when(z < depth - 1)
                    def _():
                        left(d, h).wait_recv()
                        total = value + l_buf[d, span].astype(jnp.float32)
                        held[d, span] = total.astype(held.dtype)

                left(d, h).start()

    for h in range(REDUCE_PIECES):
        span = pl.ds(h * rows, rows)
        value = base(z, h)

        @pl.when(z == 0)
        def _():
            left(z, h).wait_recv()
            out[n, span] = (value + l_buf[z, span].astype(jnp.float32)).astype(out.dtype)

        @pl.when(z == depth - 1)
        def _():
            right(z, h).wait_recv()
            out[n, span] = (value + r_buf[z, span].astype(jnp.float32)).astype(out.dtype)

        @pl.when((z > 0) & (z < depth - 1))
        def _():
            left(z, h).wait_recv()
            right(z, h).wait_recv()
            total = (
                value + l_buf[z, span].astype(jnp.float32) + r_buf[z, span].astype(jnp.float32)
            )
            out[n, span] = total.astype(out.dtype)

        sibling(h).start()

    for h in range(REDUCE_PIECES):
        for d in range(depth):
            across(d, h).wait_send()

            @pl.when(z < d)
            def _():
                right(d, h).wait_send()

            @pl.when(z > d)
            def _():
                left(d, h).wait_send()

        sibling(h).wait_send()
        copy(
            at(out, 1 - n, h), at(out, 1 - n, h), b_send.at[h], b_recv.at[h], z, y, 1 - n
        ).wait_recv()


def reduce_rows(part, count):
    depth = count // 2
    _, _, rows, width = part.shape
    dma = pltpu.SemaphoreType.DMA
    vmem = pl.BlockSpec(memory_space=pltpu.VMEM)
    pair = (depth, REDUCE_PIECES)
    block = pltpu.VMEM((depth, rows, width), part.dtype)
    return pl.pallas_call(
        functools.partial(reduce_kernel, depth),
        out_shape=jax.ShapeDtypeStruct((2, rows, width), part.dtype),
        in_specs=[vmem],
        out_specs=vmem,
        scratch_shapes=[block] * 4
        + [dma(pair)] * 6
        + [dma((REDUCE_PIECES,))] * 2,
        compiler_params=pltpu.CompilerParams(
            collective_id=1, has_side_effects=True, vmem_limit_bytes=56 * 1024 * 1024
        ),
        name="reduce_rows",
    )(part)


def slots_of(ids, expert):
    named = (ids == expert).astype(jnp.bfloat16)
    tokens = ids.shape[1]
    upper = (
        jnp.arange(tokens)[:, None] <= jnp.arange(tokens)[None, :]
    ).astype(jnp.bfloat16)
    rank = lax.dot_general(
        named, upper, (((1,), (0,)), ((), ())), preferred_element_type=jnp.float32
    ).astype(jnp.int32) - 1
    slot = jnp.where(ids == expert, rank, -1)
    return (slot[:, None, :] == jnp.arange(CAP, dtype=jnp.int32)[None, :, None]).astype(
        jnp.bfloat16
    )


def body(
    tokens, grad_out, expert_ids, routed_pre, shared_pre, w_gate, w_up, w_down, s_gate, s_up, s_down
):
    count = lax.axis_size("cross")
    node = lax.axis_index("node")
    cross = lax.axis_index("cross")
    rows, width = tokens.shape
    half = width // 2
    ids_tile = jnp.broadcast_to(expert_ids[:, 0][None, :], (8, rows))
    dy_all, ids_all, x_half = gather(grad_out, ids_tile, tokens, count)
    x_all = lax.all_gather(x_half.reshape(2 * rows, half), "cross", axis=0, tiled=True)
    blocks = 2 * count
    dy_all = dy_all.reshape(blocks, rows, width)
    ids = ids_all[:, :, 0, :].reshape(blocks, rows)
    to_slots = slots_of(ids, node)
    to_slots_b = slots_of(ids, 1 - node)
    dy_rows = (
        jnp.einsum("bst,btd->bsd", to_slots, dy_all, preferred_element_type=jnp.float32)
        .astype(jnp.bfloat16)
        .reshape(blocks * CAP, width)
    )
    sh_gate, sh_up, shared_act = silu_parts(
        shared_pre[0].astype(jnp.float32),
        shared_pre[1].astype(jnp.float32),
        right_t(dy_rows, s_down),
    )
    sh_gate = sh_gate.astype(jnp.bfloat16)
    sh_up = sh_up.astype(jnp.bfloat16)
    shared_act = shared_act.astype(jnp.bfloat16)
    mine = jnp.concatenate([sh_gate, sh_up, shared_act], axis=1)
    other = lax.ppermute(mine, "node", [(0, 1), (1, 0)])
    d_gate, d_up, _ = silu_parts(
        routed_pre[0].astype(jnp.float32),
        routed_pre[1].astype(jnp.float32),
        right_t(dy_rows, w_down[0]),
    )
    d_gate = d_gate.astype(jnp.bfloat16)
    d_up = d_up.astype(jnp.bfloat16)
    partial_in = (
        right_t(d_gate, w_gate[0])
        + right_t(d_up, w_up[0])
        + right_t(sh_gate, s_gate)
        + right_t(sh_up, s_up)
    ).astype(jnp.bfloat16)
    returned = reduce_rows(partial_in.reshape(count // 2, 2, 2 * CAP, width), count)

    own_ids = expert_ids[:, 0].reshape(1, rows)
    picks = jnp.stack([slots_of(own_ids, e)[0] for e in range(2)])
    picks = jnp.where(
        (jnp.arange(2) == node)[None, :, None, None], picks[:, None], jnp.zeros((), jnp.bfloat16)
    ).reshape(4 * CAP, rows)
    grad_tokens = left_t(picks, returned.reshape(4 * CAP, width)).astype(jnp.bfloat16)

    hidden = mine.shape[1]

    def to_tokens(one_hot, values):
        return jnp.einsum(
            "bst,bsf->btf", one_hot, values.reshape(blocks, CAP, hidden),
            preferred_element_type=jnp.float32,
        )

    by_token = (
        (to_tokens(to_slots, mine) + to_tokens(to_slots_b, other))
        .astype(jnp.bfloat16)
        .reshape(blocks * rows, hidden)
    )
    wide = hidden // 3
    dy_half = lax.dynamic_slice_in_dim(dy_all.reshape(blocks * rows, width), node * half, half, 1)
    grad_down = left_t(by_token[:, 2 * wide:], dy_half)
    grad_gate = left_t(x_all, by_token[:, :wide])
    grad_up = left_t(x_all, by_token[:, wide:2 * wide])
    return (grad_tokens, grad_gate, grad_up, grad_down)


def solution(mesh):
    in_specs = (
        P(("groups", "cross", "node"), None),
        P(("groups", "cross", "node"), None),
        P(("groups", "cross", "node"), None),
        P(None, ("groups", "node"), "cross"),
        P(None, ("groups", "node"), "cross"),
        P("node", None, "cross"),
        P("node", None, "cross"),
        P("node", "cross", None),
        P(None, "cross"),
        P(None, "cross"),
        P("cross", None),
    )
    out_specs = (
        P(("groups", "cross", "node"), None),
        P(("groups", "node"), "cross"),
        P(("groups", "node"), "cross"),
        P(("groups", "cross"), "node"),
    )
    return jax.shard_map(body, mesh=mesh, in_specs=in_specs, out_specs=out_specs, check_vma=False)
```

time: 395 us -> 255 us (0.65)
  waiting for transfers between devices: 269 us -> 0.02 us
  Pallas kernels: 0 us -> 154 us
  blocking collectives: 22.4 us -> 0 us
  matrix products: 62.4 us -> 78.1 us
  local copies, waits for them, and re-layouts: 17.2 us -> 2.42 us
  other arithmetic: 10.1 us -> 3.15 us
    all_gather x2 -> x1, waiting for transfers between devices: 164 us -> 0.01 us  [body(): lax.all_gather(x_half.reshape(2 * rows, half), 'cross', axis=0, tiled=True)]
    pallas_call x0 -> x2, Pallas kernels: none -> 154 us  [the longest x1 89.1 us: reduce_rows(): pl.pallas_call(functools.partial(reduce_kernel, depth), out_shape=jax.Sha...]
    reduce_scatter x1 -> x0, waiting for transfers between devices: 104 us -> none  [body(): lax.psum_scatter(partial_in.reshape(cross_count, experts * CAP, width), '...]
    all_to_all x3 -> x0, blocking collectives: 22.4 us -> none  [the longest x1 8.47 us: body(): lax.all_to_all(x_wide, 'node', split_axis=1, concat_axis=1, tiled=True)]
    dot_general x0 -> x7, matrix products: none -> 16.8 us  [the longest x2 10.5 us: to_tokens(): jnp.einsum('bst,bsf->btf', one_hot, values.reshape(blocks, CAP, hidden),...]
    dot_general x6, matrix products: 47 us -> 37.1 us  [right_t(): lax.dot_general(left, right, (((1,), (1,)), ((), ())), preferred_element_...]
    dot_general x3 -> x4, matrix products: 15.4 us -> 24.2 us  [left_t(): lax.dot_general(left, right, (((0,), (0,)), ((), ())), preferred_element_...]
    convert_element_type x3 -> x0, other arithmetic: 8.45 us -> none  [the longest x1 4.42 us: body(): lax.psum(grad_up.astype(jnp.bfloat16), 'node').astype(jnp.float32)]
  transfers between devices with their start and end apart: 4 -> 2, of which waited for: 3 -> 0; matrix products, arithmetic and copies ran while one was open for 17% -> 27% of each run, Pallas kernels for 0% -> 35%
where the time goes in v1:
time: 255 us; the launch traced here: 252 us
  Pallas kernels  154 us (60%)
  matrix products  78.1 us (31%)
  between operations  14.2 us (6%)
  other arithmetic  3.15 us (1%)
    pallas_call x1, Pallas kernels, reduce_rows(): pl.pallas_call(functools.partial(reduce_kernel, depth), out_shape=jax.Sha...  89.1 us
    pallas_call x1, Pallas kernels, gather(): pl.pallas_call(functools.partial(gather_kernel, depth), out_shape=(jax.Sh...  64.5 us
    dot_general x6, matrix products, right_t(): lax.dot_general(left, right, (((1,), (1,)), ((), ())), preferred_element_...  37.1 us
    dot_general x4, matrix products, left_t(): lax.dot_general(left, right, (((0,), (0,)), ((), ())), preferred_element_...  24.2 us
    dot_general x2, matrix products, to_tokens(): jnp.einsum('bst,bsf->btf', one_hot, values.reshape(blocks, CAP, hidden),...  10.5 us
    dot_general x1, matrix products, body(): jnp.einsum('bst,btd->bsd', to_slots, dy_all, preferred_element_type=jnp.f...  5.81 us
  transfers between devices with their start and end apart: 2, of which 0 were waited for; matrix products, arithmetic and copies ran while one was open for 27% of the time, Pallas kernels for 35%

profile of v1, /device:TPU:0, one launch (start us, length us, event | category | flops | bytes accessed | tf_op | source)
XLA Modules:
  0.0 251.9 jit_solution(2674099062906359795)
XLA Ops:
  7.2 1.4 broadcast_in_dim.24.ids
  8.6 64.5 %gather_rows.1 = (bf16[8,2,128,2560]{3,2,1,0:T(8,128)(2,1)}, s32[8,2,8,128]{3,2,1,0:T(8,128)}, bf16[2,128,1280]{2,1,0:T(8,128)(2,1)}) custom-call(bf16[128,2560]{1,0:T(8,128)(2,1)} %dy.1, s32[8,128]{1,0:T(8,128)} %broadcast_in_dim.24.ids, bf16[128,2560]{1,0:T(8,128)(2,1)} %x.1), custom_call_target="tpu_custom_call" | custom-call | tf_op jit(solution)/shard_map/gather_rows/pallas_call | solution.py:209
  73.1 0.9 compare_reduce_fusion
  74.1 0.1 fusion.41
  74.2 5.8 %convolution_convert_fusion = bf16[16,72,2560]{2,1,0:T(8,128)(2,1)S(1)} fusion(bf16[16,128,2560]{2,1,0:T(8,128)(2,1)} %bitcast.94, s32[16,128]{1,0:T(8,128)S(1)} %fusion.41), kind=kOutput, calls=%fused_computation.5 | convolution fusion | flops 758071296 | bytes 16392192 | tf_op jit(solution)/shard_map/bst,btd->bsd/dot_general | solution.py:435
  80.0 4.4 %multiply_convert_fusion = (bf16[1152,512]{1,0:T(8,128)(2,1)S(1)}, bf16[1152,512]{1,0:T(8,128)(2,1)S(1)}, bf16[1152,512]{1,0:T(8,128)(2,1)S(1)}) fusion(bf16[2,1152,512]{2,1,0:T(8,128)(2,1)S(1)} %copy-done.12, bf16[1152,2560]{1,0:T(8,128)(2,1)S(1)} %bitcast.96, bf16[512,2560]{1,0:T(8,128)(2,1)S(1)} %copy-done.9), kind=kOutput, calls=%fused_computation.41 | convolution fusion | flops 3029925888 | bytes 14417920 | tf_op jit(solution)/shard_map/dot_general | solution.py:25
  84.4 2.1 pad_maximum_fusion
  86.6 0.2 copy-done.5
  86.8 0.4 collective-permute-start
  87.2 0.7 copy-done.10
  87.9 3.3 %fusion.6 = f32[1152,512]{1,0:T(8,128)S(1)} fusion(bf16[1152,2560]{1,0:T(8,128)(2,1)S(1)} %bitcast.97, bf16[1,512,2560]{2,1,0:T(8,128)(2,1)S(1)} %copy-done.10), kind=kOutput, calls=%fused_computation.21 | convolution fusion | flops 3019898880 | bytes 10878976 | tf_op jit(solution)/shard_map/dot_general | solution.py:25
  91.1 7.7 %fusion.4 = f32[1152,2560]{1,0:T(8,128)} fusion(bf16[1,2560,512]{2,1,0:T(8,128)(2,1)S(1)} %copy-done, f32[1152,512]{1,0:T(8,128)S(1)} %fusion.6, bf16[2,1152,512]{2,1,0:T(8,128)(2,1)S(1)} %copy-done.4), kind=kOutput, calls=%fused_computation.19 | convolution fusion | flops 3026976768 | bytes 19136512 | tf_op jit(solution)/shard_map/dot_general | solution.py:25
  98.8 7.6 %convolution_add_fusion.2 = f32[1152,2560]{1,0:T(8,128)S(1)} fusion(f32[1152,2560]{1,0:T(8,128)} %fusion.4, bf16[1,2560,512]{2,1,0:T(8,128)(2,1)S(1)} %copy-done.2, f32[1152,512]{1,0:T(8,128)S(1)} %fusion.6, bf16[2,1152,512]{2,1,0:T(8,128)(2,1)} %param.14), kind=kOutput, calls=%fused_computation.2 | convolution fusion | flops 3026976768 | bytes 29753344 | tf_op jit(solution)/shard_map/dot_general | solution.py:25
  106.4 6.4 %convolution_add_fusion.1 = f32[1152,2560]{1,0:T(8,128)} fusion(f32[1152,2560]{1,0:T(8,128)S(1)} %convolution_add_fusion.2, bf16[1152,512]{1,0:T(8,128)(2,1)S(1)} %get-tuple-element.13, bf16[2560,512]{1,0:T(8,128)(2,1)S(1)} %copy-done.3), kind=kOutput, calls=%fused_computation.1 | convolution fusion | flops 3022848000 | bytes 27394048 | tf_op jit(solution)/shard_map/dot_general | solution.py:25
  112.8 7.8 %fusion = bf16[1152,2560]{1,0:T(8,128)(2,1)} fusion(f32[1152,2560]{1,0:T(8,128)} %convolution_add_fusion.1, bf16[1152,512]{1,0:T(8,128)(2,1)S(1)} %copy-done.6, bf16[2560,512]{1,0:T(8,128)(2,1)S(1)} %copy-done.11), kind=kOutput, calls=%fused_computation.4 | convolution fusion | flops 3025797120 | bytes 21495808 | tf_op jit(solution)/shard_map/dot_general | solution.py:25
  120.7 89.1 %reduce_rows.1 = bf16[2,144,2560]{2,1,0:T(8,128)(2,1)} custom-call(bf16[4,2,144,2560]{3,2,1,0:T(8,128)(2,1)} %bitcast.101), custom_call_target="tpu_custom_call" | custom-call | tf_op jit(solution)/shard_map/reduce_rows/pallas_call | solution.py:388
  209.8 0.1 fusion.47
  210.2 0.1 fusion.39
  210.4 2.7 %convolution_convert_fusion.1 = bf16[128,2560]{1,0:T(8,128)(2,1)} fusion(bf16[288,128]{1,0:T(8,128)(2,1)S(1)} %bitcast.104, bf16[288,2560]{1,0:T(8,128)(2,1)} %bitcast.102), kind=kOutput, calls=%fused_computation.8 | convolution fusion | flops 189071360 | bytes 2203648 | tf_op jit(solution)/shard_map/dot_general | solution.py:31
  213.1 3.8 %fusion.50 = f32[16,128,1536]{2,1,0:T(8,128)S(1)} fusion(bf16[16,72,1536]{2,1,0:T(8,128)(2,1)} %bitcast.21, s32[16,128]{1,0:T(8,128)S(1)} %fusion.41), kind=kOutput, calls=%fused_computation.71 | convolution fusion | flops 453132288 | bytes 16130048 | tf_op jit(solution)/shard_map/bst,bsf->btf/dot_general | solution.py:474
  217.0 6.6 %add_convert_fusion = bf16[16,128,1536]{2,1,0:T(8,128)(2,1)} fusion(f32[16,128,1536]{2,1,0:T(8,128)S(1)} %fusion.50, bf16[16,72,1536]{2,1,0:T(8,128)(2,1)} %bitcast.22, s32[16,128]{1,0:T(8,128)S(1)} %fusion.39), kind=kOutput, calls=%fused_computation.3 | convolution fusion | flops 459423744 | bytes 22421504 | tf_op jit(solution)/shard_map/bst,bsf->btf/dot_general | solution.py:474
  223.6 7.6 %fusion.1 = f32[512,1280]{1,0:T(8,128)} fusion(bf16[2048,2560]{1,0:T(8,128)(2,1)} %bitcast.95, s32[]{:T(128)S(6)} %select_n.39, bf16[2048,1536]{1,0:T(8,128)(2,1)} %bitcast.98), kind=kOutput, calls=%fused_computation.6 | convolution fusion | flops 2684354560 | bytes 9961476 | tf_op jit(solution)/shard_map/dot_general | solution.py:31
  231.2 7.7 %fusion.28 = f32[1280,512]{1,0:T(8,128)} fusion(bf16[2048,1280]{1,0:T(8,128)(2,1)} %all-gather.2.cloned.1.call-done, bf16[2048,1536]{1,0:T(8,128)(2,1)} %bitcast.99), kind=kOutput, calls=%fused_computation.45 | convolution fusion | flops 2684354560 | bytes 9961472 | tf_op jit(solution)/shard_map/dot_general | solution.py:31
  238.9 6.2 %fusion.26 = f32[1280,512]{1,0:T(8,128)} fusion(bf16[2048,1280]{1,0:T(8,128)(2,1)S(1)} %copy-done.8, bf16[2048,1536]{1,0:T(8,128)(2,1)} %bitcast.100), kind=kOutput, calls=%fused_computation.43 | convolution fusion | flops 2684354560 | bytes 9961472 | tf_op jit(solution)/shard_map/dot_general | solution.py:31
  (35 shorter events, 0.4 us)
Async XLA Ops:
  7.2 84.0 %copy-start = (bf16[1,2560,512]{2,1,0:T(8,128)(2,1)S(1)}, bf16[1,2560,512]{2,1,0:T(8,128)(2,1)}, u32[]{:S(2)}) copy-start(bf16[1,2560,512]{2,1,0:T(8,128)(2,1)} %param.16) | copy-start | bytes 7864324
  7.2 224.0 %all-gather.2.cloned.1.call-start = ((), (), s32[]{:S(2)}) async-start(), calls=%async_computation | async-start | bytes 5898240 | tf_op jit(solution)/shard_map/all_gather | solution.py:428
  74.2 5.8 %copy-start.9 = (bf16[512,2560]{1,0:T(8,128)(2,1)S(1)}, bf16[512,2560]{1,0:T(8,128)(2,1)}, u32[]{:S(2)}) copy-start(bf16[512,2560]{1,0:T(8,128)(2,1)} %param.21) | copy-start | bytes 7864324
  74.2 5.8 %copy-start.12 = (bf16[2,1152,512]{2,1,0:T(8,128)(2,1)S(1)}, bf16[2,1152,512]{2,1,0:T(8,128)(2,1)}, u32[]{:S(2)}) copy-start(bf16[2,1152,512]{2,1,0:T(8,128)(2,1)} %param.15) | copy-start | bytes 7077892
  84.4 2.4 copy-start.5
  84.4 3.5 %copy-start.10 = (bf16[1,512,2560]{2,1,0:T(8,128)(2,1)S(1)}, bf16[1,512,2560]{2,1,0:T(8,128)(2,1)}, u32[]{:S(2)}) copy-start(bf16[1,512,2560]{2,1,0:T(8,128)(2,1)} %param.18) | copy-start | bytes 7864324
  86.8 4.3 %copy-start.4 = (bf16[2,1152,512]{2,1,0:T(8,128)(2,1)S(1)}, bf16[2,1152,512]{2,1,0:T(8,128)(2,1)}, u32[]{:S(2)}) copy-start(bf16[2,1152,512]{2,1,0:T(8,128)(2,1)} %param.14) | copy-start | bytes 7077892
  86.8 130.2 %collective-permute-start = (bf16[1152,1536]{1,0:T(8,128)(2,1)}, bf16[1152,1536]{1,0:T(8,128)(2,1)}, u32[]{:S(2)}, u32[]{:S(2)}) collective-permute-start(bf16[1152,1536]{1,0:T(8,128)(2,1)} %pad_maximum_fusion), channel_id=1, source_target_pairs={{0,1},{1,0},{2,3},{3,2},{4,5},{5,4},{6,7},{7,6},{8,9},{9,8},{10,11... | collective-permute-start | bytes 10616840 | tf_op jit(solution)/shard_map/ppermute | solution.py:448
  91.1 7.7 %copy-start.2 = (bf16[1,2560,512]{2,1,0:T(8,128)(2,1)S(1)}, bf16[1,2560,512]{2,1,0:T(8,128)(2,1)}, u32[]{:S(2)}) copy-start(bf16[1,2560,512]{2,1,0:T(8,128)(2,1)} %param.17) | copy-start | bytes 7864324
  98.8 7.6 %copy-start.3 = (bf16[2560,512]{1,0:T(8,128)(2,1)S(1)}, bf16[2560,512]{1,0:T(8,128)(2,1)}, u32[]{:S(2)}) copy-start(bf16[2560,512]{1,0:T(8,128)(2,1)} %param.19) | copy-start | bytes 7864324
  106.4 6.4 %copy-start.6 = (bf16[1152,512]{1,0:T(8,128)(2,1)S(1)}, bf16[1152,512]{1,0:T(8,128)(2,1)}, u32[]{:S(2)}) copy-start(bf16[1152,512]{1,0:T(8,128)(2,1)} %copy-done.5) | copy-start | bytes 3538948
  106.4 6.4 %copy-start.11 = (bf16[2560,512]{1,0:T(8,128)(2,1)S(1)}, bf16[2560,512]{1,0:T(8,128)(2,1)}, u32[]{:S(2)}) copy-start(bf16[2560,512]{1,0:T(8,128)(2,1)} %param.20) | copy-start | bytes 7864324
  120.7 89.2 %copy-start.7 = (s32[128,1]{0,1:T(1,128)S(1)}, s32[128,1]{0,1:T(1,128)}, u32[]{:S(2)}) copy-start(s32[128,1]{0,1:T(1,128)} %param.13) | copy-start | bytes 1540
  231.2 7.7 %copy-start.8 = (bf16[2048,1280]{1,0:T(8,128)(2,1)S(1)}, bf16[2048,1280]{1,0:T(8,128)(2,1)}, u32[]{:S(2)}) copy-start(bf16[2048,1280]{1,0:T(8,128)(2,1)} %all-gather.2.cloned.1.call-done) | copy-start | bytes 15728644
  238.9 6.2 %copy-start.1 = (bf16[1,2560,512]{2,1,0:T(8,128)(2,1)S(1)}, bf16[1,2560,512]{2,1,0:T(8,128)(2,1)}, u32[]{:S(2)}) copy-start(bf16[1,2560,512]{2,1,0:T(8,128)(2,1)} %param.16) | copy-start | bytes 7864324
Sparse Core Ops, SparseCore 0:
  73.3 112.1 all-gather.1

commit v2 on v1

--- a/solution.py
+++ b/solution.py
@@ -10,7 +10,6 @@
 CAP = 72
 MESH = pl.DeviceIdType.MESH
 GATHER_PIECES = 2
-REDUCE_PIECES = 3
 
 
 def silu_parts(pre_gate, pre_up, grad_hidden):
@@ -231,173 +230,90 @@
     )(dy, ids, x)
 
 
-def reduce_kernel(
-    depth, part, out, y_buf, r_buf, l_buf, held,
-    y_send, y_recv, r_send, r_recv, l_send, l_recv, b_send, b_recv,
-):
-    z, y, n = place(depth)
-    rows = part.shape[2] // REDUCE_PIECES
-    greet(z, y, n, depth)
-
-    def at(ref, d, h):
-        return ref.at[d, pl.ds(h * rows, rows)]
-
-    def copy(src, dst, send_sem, recv_sem, zz, yy, nn):
-        return pltpu.make_async_remote_copy(
-            src_ref=src, dst_ref=dst, send_sem=send_sem, recv_sem=recv_sem,
-            device_id={"cross": zz * 2 + yy, "node": nn}, device_id_type=MESH,
-        )
-
-    def across(d, h):
-        return copy(
-            part.at[d, 1 - y, pl.ds(h * rows, rows)], at(y_buf, d, h),
-            y_send.at[d, h], y_recv.at[d, h], z, 1 - y, n,
-        )
-
-    def right(d, h):
-        return copy(
-            at(held, d, h), at(r_buf, d, h), r_send.at[d, h], r_recv.at[d, h], z + 1, y, n
-        )
-
-    def left(d, h):
-        return copy(
-            at(held, d, h), at(l_buf, d, h), l_send.at[d, h], l_recv.at[d, h], z - 1, y, n
-        )
-
-    def sibling(h):
-        return copy(
-            at(out, n, h), at(out, n, h), b_send.at[h], b_recv.at[h], z, y, 1 - n
-        )
-
-    def walk(s, act):
-        if s == 0:
-            act(z)
-        else:
-            @pl.when(z + s < depth)
-            def _():
-                act(z + s)
-
-            @pl.when(z - s >= 0)
-            def _():
-                act(z - s)
-
-    def begin(s):
-        for h in range(REDUCE_PIECES):
-            walk(s, lambda d, h=h: across(d, h).start())
-
-    def base(d, h):
-        across(d, h).wait_recv()
-        return part[d, y, pl.ds(h * rows, rows)].astype(jnp.float32) + y_buf[
-            d, pl.ds(h * rows, rows)
-        ].astype(jnp.float32)
-
-    begin(depth - 1)
-    for s in range(depth - 1, 0, -1):
-        begin(s - 1)
-        for h in range(REDUCE_PIECES):
-            span = pl.ds(h * rows, rows)
-
-            @pl.when(z + s < depth)
-            def _():
-                d = z + s
-                value = base(d, h)
-                if s == depth - 1:
-                    held[d, span] = value.astype(held.dtype)
-                else:
-                    @pl.when(z == 0)
-                    def _():
-                        held[d, span] = value.astype(held.dtype)
-
-                    @pl.when(z > 0)
-                    def _():
-                        right(d, h).wait_recv()
-                        total = value + r_buf[d, span].astype(jnp.float32)
-                        held[d, span] = total.astype(held.dtype)
-
-                right(d, h).start()
-
-            @pl.when(z - s >= 0)
-            def _():
-                d = z - s
-                value = base(d, h)
-                if s == depth - 1:
-                    held[d, span] = value.astype(held.dtype)
-                else:
-                    @pl.when(z == depth - 1)
-                    def _():
-                        held[d, span] = value.astype(held.dtype)
-
-                    @pl.when(z < depth - 1)
-                    def _():
-                        left(d, h).wait_recv()
-                        total = value + l_buf[d, span].astype(jnp.float32)
-                        held[d, span] = total.astype(held.dtype)
-
-                left(d, h).start()
-
-    for h in range(REDUCE_PIECES):
-        span = pl.ds(h * rows, rows)
-        value = base(z, h)
-
-        @pl.when(z == 0)
-        def _():
-            left(z, h).wait_recv()
-            out[n, span] = (value + l_buf[z, span].astype(jnp.float32)).astype(out.dtype)
-
-        @pl.when(z == depth - 1)
-        def _():
-            right(z, h).wait_recv()
-            out[n, span] = (value + r_buf[z, span].astype(jnp.float32)).astype(out.dtype)
-
-        @pl.when((z > 0) & (z < depth - 1))
-        def _():
-            left(z, h).wait_recv()
-            right(z, h).wait_recv()
-            total = (
-                value + l_buf[z, span].astype(jnp.float32) + r_buf[z, span].astype(jnp.float32)
-            )
-            out[n, span] = total.astype(out.dtype)
-
-        sibling(h).start()
-
-    for h in range(REDUCE_PIECES):
-        for d in range(depth):
-            across(d, h).wait_send()
-
-            @pl.when(z < d)
-            def _():
-                right(d, h).wait_send()
-
-            @pl.when(z > d)
-            def _():
-                left(d, h).wait_send()
-
-        sibling(h).wait_send()
-        copy(
-            at(out, 1 - n, h), at(out, 1 - n, h), b_send.at[h], b_recv.at[h], z, y, 1 - n
-        ).wait_recv()
+def line_pairs(depth, step, s):
+    pairs = []
+    for z in range(depth):
+        if 0 <= z + step * s < depth:
+            pairs += [(z * 2 + y, (z + step) * 2 + y) for y in range(2)]
+    return pairs
+
+
+def across_pairs(depth, step, s):
+    return [
+        (z * 2 + y, z * 2 + 1 - y)
+        for z in range(depth)
+        if 0 <= z + step * s < depth
+        for y in range(2)
+    ]
+
+
+def gather_step(x, count, until, came):
+    depth = count // 2
+    for step in (1, -1):
+        start = 1 + max([s for (k, s) in came if k == step], default=0)
+        block = came[step, start - 1][0] if start > 1 else x
+        for s in range(start, min(until + 1, depth)):
+            pairs = [
+                (z * 2 + y, (z + step) * 2 + y)
+                for z in range(depth)
+                if 0 <= z + step < depth and 0 <= z - step * (s - 1) < depth
+                for y in range(2)
+            ]
+            block = lax.ppermute(block, "cross", pairs)
+            came[step, s] = (block, None)
+    return came
+
+
+def held_until(came, s, *values):
+    right, left, *values = lax.optimization_barrier(
+        (came[1, s][0], came[-1, s][0]) + values
+    )
+    depth = lax.axis_size("cross") // 2
+    for step, block in ((1, right), (-1, left)):
+        over = lax.ppermute(block, "cross", across_pairs(depth, -step, s))
+        came[step, s] = (block, over)
+    return values
+
+
+def by_distance(x, first, came, count):
+    depth = count // 2
+    out = [x, first]
+    for s in range(1, depth):
+        for j in range(2):
+            out.append(came[-1, s][j] + came[1, depth - s][j])
+    return jnp.concatenate(out, axis=0)
 
 
 def reduce_rows(part, count):
     depth = count // 2
-    _, _, rows, width = part.shape
-    dma = pltpu.SemaphoreType.DMA
-    vmem = pl.BlockSpec(memory_space=pltpu.VMEM)
-    pair = (depth, REDUCE_PIECES)
-    block = pltpu.VMEM((depth, rows, width), part.dtype)
-    return pl.pallas_call(
-        functools.partial(reduce_kernel, depth),
-        out_shape=jax.ShapeDtypeStruct((2, rows, width), part.dtype),
-        in_specs=[vmem],
-        out_specs=vmem,
-        scratch_shapes=[block] * 4
-        + [dma(pair)] * 6
-        + [dma((REDUCE_PIECES,))] * 2,
-        compiler_params=pltpu.CompilerParams(
-            collective_id=1, has_side_effects=True, vmem_limit_bytes=56 * 1024 * 1024
-        ),
-        name="reduce_rows",
-    )(part)
+    z, y = lax.div(lax.axis_index("cross"), 2), lax.rem(lax.axis_index("cross"), 2)
+    f32 = jnp.float32
+
+    def pick(d, column):
+        return lax.dynamic_slice(
+            part, (d, column, 0, 0), (1, 1) + part.shape[2:]
+        ).reshape(part.shape[2:])
+
+    def base(step, s):
+        d = jnp.clip(z + step * s, 0, depth - 1)
+        got = lax.ppermute(pick(d, 1 - y), "cross", across_pairs(depth, step, s))
+        return pick(d, y).astype(f32) + got.astype(f32)
+
+    moving = {1: None, -1: None}
+    for s in range(depth - 1, 0, -1):
+        for step in (1, -1):
+            total = base(step, s)
+            if moving[step] is not None:
+                total = total + moving[step].astype(f32)
+            moving[step] = lax.ppermute(
+                total.astype(part.dtype), "cross", line_pairs(depth, step, s)
+            )
+    total = base(1, 0) + moving[1].astype(f32) + moving[-1].astype(f32)
+    total = total.astype(part.dtype)
+    other = lax.ppermute(total, "node", [(0, 1), (1, 0)])
+    first = jnp.where(lax.axis_index("node") == 0, total, other)
+    second = jnp.where(lax.axis_index("node") == 0, other, total)
+    return jnp.stack([first, second])
 
 
 def slots_of(ids, expert):
@@ -425,7 +341,10 @@
     half = width // 2
     ids_tile = jnp.broadcast_to(expert_ids[:, 0][None, :], (8, rows))
     dy_all, ids_all, x_half = gather(grad_out, ids_tile, tokens, count)
-    x_all = lax.all_gather(x_half.reshape(2 * rows, half), "cross", axis=0, tiled=True)
+    x_block = x_half.reshape(2 * rows, half)
+    depth = count // 2
+    across = lax.ppermute(x_block, "cross", across_pairs(depth, 1, 0))
+    came = gather_step(x_block, count, 1, {})
     blocks = 2 * count
     dy_all = dy_all.reshape(blocks, rows, width)
     ids = ids_all[:, :, 0, :].reshape(blocks, rows)
@@ -453,12 +372,23 @@
     )
     d_gate = d_gate.astype(jnp.bfloat16)
     d_up = d_up.astype(jnp.bfloat16)
-    partial_in = (
-        right_t(d_gate, w_gate[0])
-        + right_t(d_up, w_up[0])
-        + right_t(sh_gate, s_gate)
-        + right_t(sh_up, s_up)
-    ).astype(jnp.bfloat16)
+    d_gate, d_up = held_until(came, 1, d_gate, d_up)
+    gather_step(x_block, count, 2, came)
+    partial_in = right_t(d_gate, w_gate[0]) + right_t(d_up, w_up[0])
+    (partial_in,) = held_until(came, 2, partial_in)
+    gather_step(x_block, count, depth - 1, came)
+    partial_in = (partial_in + right_t(sh_gate, s_gate) + right_t(sh_up, s_up)).astype(
+        jnp.bfloat16
+    )
+    right, left, partial_in = lax.optimization_barrier(
+        (came[1, 1][1], came[-1, 1][1], partial_in)
+    )
+    came[1, 1] = (came[1, 1][0], right)
+    came[-1, 1] = (came[-1, 1][0], left)
+    (partial_in,) = held_until(came, 3, partial_in)
+    for s in range(4, depth):
+        held_until(came, s)
+    x_all = by_distance(x_block, across, came, count)
     returned = reduce_rows(partial_in.reshape(count // 2, 2, 2 * CAP, width), count)
 
     own_ids = expert_ids[:, 0].reshape(1, rows)
@@ -484,8 +414,15 @@
     wide = hidden // 3
     dy_half = lax.dynamic_slice_in_dim(dy_all.reshape(blocks * rows, width), node * half, half, 1)
     grad_down = left_t(by_token[:, 2 * wide:], dy_half)
-    grad_gate = left_t(x_all, by_token[:, :wide])
-    grad_up = left_t(x_all, by_token[:, wide:2 * wide])
+    z, y = lax.div(cross, 2), lax.rem(cross, 2)
+    far = jnp.arange(count, dtype=jnp.int32)
+    order = lax.rem(z + far // 2, count // 2) * 2 + jnp.where(far % 2 == 0, y, 1 - y)
+    near = jnp.take(
+        by_token[:, :2 * wide].reshape(count, 2 * rows, 2 * wide), order, axis=0,
+        mode="clip",
+    ).reshape(blocks * rows, 2 * wide)
+    grad_gate = left_t(x_all, near[:, :wide])
+    grad_up = left_t(x_all, near[:, wide:])
     return (grad_tokens, grad_gate, grad_up, grad_down)
 
 

time: 255 us -> 292 us (1.15)
  Pallas kernels: 154 us -> 64.5 us
  waiting for transfers between devices: 0.02 us -> 67 us
  starting transfers between devices: 0.42 us -> 41.9 us
  other arithmetic: 3.15 us -> 31.7 us
  local copies, waits for them, and re-layouts: 2.42 us -> 19.1 us
  between operations: 14.2 us -> 1.16 us
  matrix products: 78.1 us -> 65.1 us
    pallas_call x1 -> x0, Pallas kernels: 89.1 us -> none  [reduce_rows(): pl.pallas_call(functools.partial(reduce_kernel, depth), out_shape=jax.Sha...]
    ppermute x0 -> x27, waiting for transfers between devices: none -> 67 us  [the longest x7 34.2 us: base(): got = lax.ppermute(pick(d, 1 - y), 'cross', across_pairs(depth, step, s))]
    ppermute x0 -> x27, starting transfers between devices: none -> 41.8 us  [the longest x6 12.3 us: held_until(): over = lax.ppermute(block, 'cross', across_pairs(depth, -step, s))]
    convert_element_type x0 -> x7, other arithmetic: none -> 15.6 us  [the longest x1 9.1 us: body(): (partial_in + right_t(sh_gate, s_gate) + right_t(sh_up, s_up)).astype(jnp...]
    unnamed x0 -> x6, other arithmetic: none -> 9.54 us
    unnamed x26 -> x42, local copies, waits for them, and re-layouts: 0.98 us -> 8.63 us
    dot_general x4, matrix products: 24.2 us -> 17.9 us  [left_t(): lax.dot_general(left, right, (((0,), (0,)), ((), ())), preferred_element_...]
    dot_general x6, matrix products: 37.1 us -> 31.6 us  [right_t(): lax.dot_general(left, right, (((1,), (1,)), ((), ())), preferred_element_...]
  transfers between devices with their start and end apart: 2 -> 28, of which waited for: 0 -> 8; matrix products, arithmetic and copies ran while one was open for 27% -> 37% of each run, Pallas kernels for 35% -> 0%
where the time goes in v2:
time: 292 us; the launch traced here: 290 us
  waiting for transfers between devices  67 us (23%)
  matrix products  65.1 us (22%)
  Pallas kernels  64.5 us (22%)
  starting transfers between devices  41.9 us (14%)
  other arithmetic  31.7 us (11%)
  local copies, waits for them, and re-layouts  19.1 us (7%)
    pallas_call x1, Pallas kernels, gather(): pl.pallas_call(functools.partial(gather_kernel, depth), out_shape=(jax.Sh...  64.5 us
    ppermute x7, waiting for transfers between devices, base(): got = lax.ppermute(pick(d, 1 - y), 'cross', across_pairs(depth, step, s))  34.2 us
    dot_general x6, matrix products, right_t(): lax.dot_general(left, right, (((1,), (1,)), ((), ())), preferred_element_...  31.6 us
    dot_general x4, matrix products, left_t(): lax.dot_general(left, right, (((0,), (0,)), ((), ())), preferred_element_...  17.9 us
    ppermute x6, waiting for transfers between devices, gather_step(): block = lax.ppermute(block, 'cross', pairs)  15.3 us
    ppermute x6, starting transfers between devices, held_until(): over = lax.ppermute(block, 'cross', across_pairs(depth, -step, s))  12.3 us
    ppermute x7, starting transfers between devices, base(): got = lax.ppermute(pick(d, 1 - y), 'cross', across_pairs(depth, step, s))  10.7 us
    ppermute x6, starting transfers between devices, gather_step(): block = lax.ppermute(block, 'cross', pairs)  10.4 us
  transfers between devices with their start and end apart: 28, of which 8 were waited for; matrix products, arithmetic and copies ran while one was open for 37% of the time, Pallas kernels for 0%

profile of v2, /device:TPU:0, one launch (start us, length us, event | category | flops | bytes accessed | tf_op | source)
XLA Modules:
  0.0 290.4 jit_solution(14612477183124256633)
XLA Ops:
  2.0 64.5 %gather_rows.1 = (bf16[8,2,128,2560]{3,2,1,0:T(8,128)(2,1)}, s32[8,2,8,128]{3,2,1,0:T(8,128)}, bf16[2,128,1280]{2,1,0:T(8,128)(2,1)}) custom-call(bf16[128,2560]{1,0:T(8,128)(2,1)} %dy.1, s32[8,128]{1,0:T(8,128)} %broadcast_in_dim.31.ids, bf16[128,2560]{1,0:T(8,128)(2,1)} %x.1), custom_call_target="tpu_custom_call" | custom-call | tf_op jit(solution)/shard_map/gather_rows/pallas_call | solution.py:208
  66.5 4.4 %collective-permute-start = (bf16[256,1280]{1,0:T(8,128)(2,1)}, bf16[256,1280]{1,0:T(8,128)(2,1)}, u32[]{:S(2)}, u32[]{:S(2)}) collective-permute-start(bf16[256,1280]{1,0:T(8,128)(2,1)} %bitcast.150), channel_id=1, source_target_pairs={{0,4},{2,6},{4,8},{6,10},{8,12},{10,14},{1,5},{3,7},{5,9},{7,11},{... | collective-permute-start | bytes 1966088 | tf_op jit(solution)/shard_map/ppermute | solution.py:262
  77.9 5.8 %convolution_convert_fusion = bf16[16,72,2560]{2,1,0:T(8,128)(2,1)S(1)} fusion(bf16[16,128,2560]{2,1,0:T(8,128)(2,1)} %bitcast.139, s32[16,128]{1,0:T(8,128)S(1)} %fusion.45), kind=kOutput, calls=%fused_computation.4 | convolution fusion | flops 758071296 | bytes 16392192 | tf_op jit(solution)/shard_map/bst,btd->bsd/dot_general | solution.py:354
  83.8 5.2 %fusion.18 = (bf16[1152,512]{1,0:T(8,128)(2,1)}, bf16[1152,512]{1,0:T(8,128)(2,1)}) fusion(bf16[2,1152,512]{2,1,0:T(8,128)(2,1)S(1)} %copy-done.15, bf16[1152,2560]{1,0:T(8,128)(2,1)S(1)} %bitcast.144, bf16[1,512,2560]{2,1,0:T(8,128)(2,1)S(1)} %copy-done.11), kind=kOutput, calls=%fused_computation.33 | convolution fusion | flops 3028746240 | bytes 13238272 | tf_op jit(solution)/shard_map/dot_general | solution.py:24
  88.9 5.4 %fusion.9 = (bf16[1152,512]{1,0:T(8,128)(2,1)S(1)}, bf16[1152,512]{1,0:T(8,128)(2,1)S(1)}, bf16[1152,512]{1,0:T(8,128)(2,1)}) fusion(bf16[2,1152,512]{2,1,0:T(8,128)(2,1)S(1)} %copy-done.16, bf16[1152,2560]{1,0:T(8,128)(2,1)S(1)} %bitcast.145, bf16[512,2560]{1,0:T(8,128)(2,1)S(1)} %copy-done.12), kind=kOutput, calls=%fused_computation.24 | convolution fusion | flops 3029925888 | bytes 14417920 | tf_op jit(solution)/shard_map/dot_general | solution.py:24
  94.3 6.1 %fusion.73 = f32[1152,2560]{1,0:T(8,128)} fusion(bf16[1152,512]{1,0:T(8,128)(2,1)S(1)} %get-tuple-element.48, bf16[2560,512]{1,0:T(8,128)(2,1)S(1)} %copy-done), kind=kOutput, calls=%fused_computation.138 | convolution fusion | flops 3019898880 | bytes 15597568 | tf_op jit(solution)/shard_map/dot_general | solution.py:24
  100.5 6.1 %fusion.72 = f32[1152,2560]{1,0:T(8,128)} fusion(bf16[1152,512]{1,0:T(8,128)(2,1)S(1)} %get-tuple-element.47, bf16[2560,512]{1,0:T(8,128)(2,1)S(1)} %copy-done.13), kind=kOutput, calls=%fused_computation.137 | convolution fusion | flops 3019898880 | bytes 15597568 | tf_op jit(solution)/shard_map/dot_general | solution.py:24
  114.0 3.6 %collective-permute-start.7 = (bf16[256,1280]{1,0:T(8,128)(2,1)}, bf16[256,1280]{1,0:T(8,128)(2,1)}, u32[]{:S(2)}, u32[]{:S(2)}) collective-permute-start(bf16[256,1280]{1,0:T(8,128)(2,1)} %collective-permute-done.1), channel_id=1, source_target_pairs={{0,2},{2,0},{4,6},{6,4},{8,10},{10,8},{1,3},{3,1},{5,7},{7,5},{9,1... | collective-permute-start | bytes 1966088 | tf_op jit(solution)/shard_map/ppermute | solution.py:273
  120.9 5.6 %convolution_add_fusion = f32[1152,2560]{1,0:T(8,128)S(1)} fusion(f32[1152,2560]{1,0:T(8,128)S(1)} %fusion.2, bf16[1152,512]{1,0:T(8,128)(2,1)} %get-tuple-element.25, bf16[1,2560,512]{2,1,0:T(8,128)(2,1)} %param.16), kind=kOutput, calls=%fused_computation.1 | convolution fusion | flops 3022848000 | bytes 27394048 | tf_op jit(solution)/shard_map/dot_general | solution.py:24
  126.5 8.8 %collective-permute-done.3 = bf16[256,1280]{1,0:T(8,128)(2,1)} collective-permute-done((bf16[256,1280]{1,0:T(8,128)(2,1)}, bf16[256,1280]{1,0:T(8,128)(2,1)}, u32[]{:S(2)}, u32[]{:S(2)}) %collective-permute-start.3) | collective-permute-done | bytes 655392 | tf_op jit(solution)/shard_map/ppermute | solution.py:262
  137.4 9.1 %add_convert_fusion.1 = bf16[1152,2560]{1,0:T(8,128)(2,1)S(1)} fusion(f32[1152,2560]{1,0:T(8,128)} %fusion.73, f32[1152,2560]{1,0:T(8,128)S(1)} %convolution_add_fusion, f32[1152,2560]{1,0:T(8,128)} %fusion.72), kind=kLoop, calls=%fused_computation.3 | loop fusion | flops 8847360 | bytes 41287680 | tf_op jit(solution)/shard_map/convert_element_type | solution.py:380
  146.6 6.5 %collective-permute-done.5 = bf16[256,1280]{1,0:T(8,128)(2,1)S(1)} collective-permute-done((bf16[256,1280]{1,0:T(8,128)(2,1)}, bf16[256,1280]{1,0:T(8,128)(2,1)S(1)}, u32[]{:S(2)}, u32[]{:S(2)}) %collective-permute-start.5) | collective-permute-done | bytes 655392 | tf_op jit(solution)/shard_map/ppermute | solution.py:262
  157.0 3.8 %fusion.52 = f32[16,128,1536]{2,1,0:T(8,128)S(1)} fusion(bf16[16,72,1536]{2,1,0:T(8,128)(2,1)} %bitcast.37, s32[16,128]{1,0:T(8,128)S(1)} %fusion.45), kind=kOutput, calls=%fused_computation.98 | convolution fusion | flops 453132288 | bytes 16130048 | tf_op jit(solution)/shard_map/bst,bsf->btf/dot_general | solution.py:404
  162.8 3.4 %collective-permute-start.24 = (bf16[256,1280]{1,0:T(8,128)(2,1)}, bf16[256,1280]{1,0:T(8,128)(2,1)S(1)}, u32[]{:S(2)}, u32[]{:S(2)}) collective-permute-start(bf16[256,1280]{1,0:T(8,128)(2,1)} %collective-permute-done.3), channel_id=1, source_target_pairs={{0,2},{2,0},{4,6},{6,4},{1,3},{3,1},{5,7},{7,5},{16,18},{18,16},{2... | collective-permute-start | bytes 1966088 | tf_op jit(solution)/shard_map/ppermute | solution.py:273
  169.4 6.5 %collective-permute-done.11 = bf16[144,2560]{1,0:T(8,128)(2,1)S(1)} collective-permute-done((bf16[144,2560]{1,0:T(8,128)(2,1)S(1)}, bf16[144,2560]{1,0:T(8,128)(2,1)S(1)}, u32[]{:S(2)}, u32[]{:S(2)}) %collective-permute-start.11) | collective-permute-done | bytes 737312 | tf_op jit(solution)/shard_map/ppermute | solution.py:299
  182.3 19.8 %collective-permute-done.10 = bf16[144,2560]{1,0:T(8,128)(2,1)S(1)} collective-permute-done((bf16[144,2560]{1,0:T(8,128)(2,1)S(1)}, bf16[144,2560]{1,0:T(8,128)(2,1)S(1)}, u32[]{:S(2)}, u32[]{:S(2)}) %collective-permute-start.10) | collective-permute-done | bytes 737312 | tf_op jit(solution)/shard_map/ppermute | solution.py:299
  210.8 8.0 %collective-permute-done.9 = bf16[144,2560]{1,0:T(8,128)(2,1)S(1)} collective-permute-done((bf16[144,2560]{1,0:T(8,128)(2,1)S(1)}, bf16[144,2560]{1,0:T(8,128)(2,1)S(1)}, u32[]{:S(2)}, u32[]{:S(2)}) %collective-permute-start.9) | collective-permute-done | bytes 737312 | tf_op jit(solution)/shard_map/ppermute | solution.py:299
  227.1 9.8 %collective-permute-done.26 = bf16[256,1280]{1,0:T(8,128)(2,1)S(1)} collective-permute-done((bf16[256,1280]{1,0:T(8,128)(2,1)S(1)}, bf16[256,1280]{1,0:T(8,128)(2,1)S(1)}, u32[]{:S(2)}, u32[]{:S(2)}) %collective-permute-start.26) | collective-permute-done | bytes 655392 | tf_op jit(solution)/shard_map/ppermute | solution.py:273
  244.0 4.0 %add_convert_fusion = bf16[16,128,1536]{2,1,0:T(8,128)(2,1)S(1)} fusion(f32[16,128,1536]{2,1,0:T(8,128)S(1)} %fusion.52, bf16[16,72,1536]{2,1,0:T(8,128)(2,1)} %bitcast.149, s32[16,128]{1,0:T(8,128)S(1)} %fusion.43), kind=kOutput, calls=%fused_computation.2 | convolution fusion | flops 459423744 | bytes 22421504 | tf_op jit(solution)/shard_map/bst,bsf->btf/dot_general | solution.py:404
  253.3 4.9 %gather_fusion = bf16[8,256,1024]{2,1,0:T(8,128)(2,1)} fusion(bf16[8,256,1024]{2,1,0:T(8,128)(2,1)} %bitcast.143, s32[1024]{0:T(1024)S(1)} %pad_clamp_fusion), kind=kCustom, calls=%fused_computation | custom fusion | bytes 8388640 | tf_op jit(solution)/shard_map/jit(_take)/gather | solution.py:420
  258.2 7.7 %fusion = f32[512,1280]{1,0:T(8,128)} fusion(bf16[2048,2560]{1,0:T(8,128)(2,1)} %bitcast.140, s32[]{:T(128)S(6)} %select_n.128, bf16[2048,1536]{1,0:T(8,128)(2,1)} %bitcast.142), kind=kOutput, calls=%fused_computation.5 | convolution fusion | flops 2684354560 | bytes 9961476 | tf_op jit(solution)/shard_map/dot_general | solution.py:30
  270.5 4.4 %fusion.27 = f32[1280,512]{1,0:T(8,128)} fusion(bf16[2048,1280]{1,0:T(8,128)(2,1)S(1)} %bitcast.156, bf16[2048,1024]{1,0:T(8,128)(2,1)S(1)} %bitcast.147), kind=kOutput, calls=%fused_computation.44 | convolution fusion | flops 2684354560 | bytes 9961472 | tf_op jit(solution)/shard_map/dot_general | solution.py:30
  276.2 6.3 %collective-permute-done.20 = bf16[144,2560]{1,0:T(8,128)(2,1)S(1)} collective-permute-done((bf16[144,2560]{1,0:T(8,128)(2,1)S(1)}, bf16[144,2560]{1,0:T(8,128)(2,1)S(1)}, u32[]{:S(2)}, u32[]{:S(2)}) %collective-permute-start.20) | collective-permute-done | bytes 737312 | tf_op jit(solution)/shard_map/ppermute | solution.py:308
  284.3 4.4 %fusion.25 = f32[1280,512]{1,0:T(8,128)} fusion(bf16[2048,1280]{1,0:T(8,128)(2,1)S(1)} %bitcast.156, bf16[2048,1024]{1,0:T(8,128)(2,1)S(1)} %bitcast.148), kind=kOutput, calls=%fused_computation.42 | convolution fusion | flops 2684354560 | bytes 9961472 | tf_op jit(solution)/shard_map/dot_general | solution.py:30
  (123 shorter events, 75.2 us)
Async XLA Ops:
  66.5 43.2 %collective-permute-start = (bf16[256,1280]{1,0:T(8,128)(2,1)}, bf16[256,1280]{1,0:T(8,128)(2,1)}, u32[]{:S(2)}, u32[]{:S(2)}) collective-permute-start(bf16[256,1280]{1,0:T(8,128)(2,1)} %bitcast.150), channel_id=1, source_target_pairs={{0,4},{2,6},{4,8},{6,10},{8,12},{10,14},{1,5},{3,7},{5,9},{7,11},{... | collective-permute-start | bytes 1966088 | tf_op jit(solution)/shard_map/ppermute | solution.py:262
  70.9 38.8 %collective-permute-start.1 = (bf16[256,1280]{1,0:T(8,128)(2,1)}, bf16[256,1280]{1,0:T(8,128)(2,1)}, u32[]{:S(2)}, u32[]{:S(2)}) collective-permute-start(bf16[256,1280]{1,0:T(8,128)(2,1)} %bitcast.151), channel_id=1, source_target_pairs={{4,0},{6,2},{8,4},{10,6},{12,8},{14,10},{5,1},{7,3},{9,5},{11,7},{... | collective-permute-start | bytes 1966088 | tf_op jit(solution)/shard_map/ppermute | solution.py:262
  72.2 88.6 %collective-permute-start.22 = (bf16[256,1280]{1,0:T(8,128)(2,1)}, bf16[256,1280]{1,0:T(8,128)(2,1)}, u32[]{:S(2)}, u32[]{:S(2)}) collective-permute-start(bf16[256,1280]{1,0:T(8,128)(2,1)} %bitcast.152), channel_id=1, source_target_pairs={{0,2},{2,0},{4,6},{6,4},{8,10},{10,8},{12,14},{14,12},{1,3},{3,1},... | collective-permute-start | bytes 1966088 | tf_op jit(solution)/shard_map/ppermute | solution.py:346
  109.7 16.8 %collective-permute-start.2 = (bf16[256,1280]{1,0:T(8,128)(2,1)}, bf16[256,1280]{1,0:T(8,128)(2,1)}, u32[]{:S(2)}, u32[]{:S(2)}) collective-permute-start(bf16[256,1280]{1,0:T(8,128)(2,1)} %collective-permute-done), channel_id=1, source_target_pairs={{4,8},{6,10},{8,12},{10,14},{5,9},{7,11},{9,13},{11,15},{20,24},{2... | collective-permute-start | bytes 1966088 | tf_op jit(solution)/shard_map/ppermute | solution.py:262
  111.2 35.3 %collective-permute-start.6 = (bf16[256,1280]{1,0:T(8,128)(2,1)}, bf16[256,1280]{1,0:T(8,128)(2,1)}, u32[]{:S(2)}, u32[]{:S(2)}) collective-permute-start(bf16[256,1280]{1,0:T(8,128)(2,1)} %collective-permute-done), channel_id=1, source_target_pairs={{4,6},{6,4},{8,10},{10,8},{12,14},{14,12},{5,7},{7,5},{9,11},{11,9... | collective-permute-start | bytes 1966088 | tf_op jit(solution)/shard_map/ppermute | solution.py:273
  112.7 22.6 %collective-permute-start.3 = (bf16[256,1280]{1,0:T(8,128)(2,1)}, bf16[256,1280]{1,0:T(8,128)(2,1)}, u32[]{:S(2)}, u32[]{:S(2)}) collective-permute-start(bf16[256,1280]{1,0:T(8,128)(2,1)} %collective-permute-done.1), channel_id=1, source_target_pairs={{4,0},{6,2},{8,4},{10,6},{5,1},{7,3},{9,5},{11,7},{20,16},{22,18},... | collective-permute-start | bytes 1966088 | tf_op jit(solution)/shard_map/ppermute | solution.py:262
  114.0 32.6 %collective-permute-start.7 = (bf16[256,1280]{1,0:T(8,128)(2,1)}, bf16[256,1280]{1,0:T(8,128)(2,1)}, u32[]{:S(2)}, u32[]{:S(2)}) collective-permute-start(bf16[256,1280]{1,0:T(8,128)(2,1)} %collective-permute-done.1), channel_id=1, source_target_pairs={{0,2},{2,0},{4,6},{6,4},{8,10},{10,8},{1,3},{3,1},{5,7},{7,5},{9,1... | collective-permute-start | bytes 1966088 | tf_op jit(solution)/shard_map/ppermute | solution.py:273
  136.1 17.1 %collective-permute-start.5 = (bf16[256,1280]{1,0:T(8,128)(2,1)}, bf16[256,1280]{1,0:T(8,128)(2,1)S(1)}, u32[]{:S(2)}, u32[]{:S(2)}) collective-permute-start(bf16[256,1280]{1,0:T(8,128)(2,1)} %collective-permute-done.3), channel_id=1, source_target_pairs={{4,0},{6,2},{5,1},{7,3},{20,16},{22,18},{21,17},{23,19}} | collective-permute-start | bytes 1966088 | tf_op jit(solution)/shard_map/ppermute | solution.py:262
  146.5 95.7 %collective-permute-start.27 = (bf16[1152,1536]{1,0:T(8,128)(2,1)}, bf16[1152,1536]{1,0:T(8,128)(2,1)S(1)}, u32[]{:S(2)}, u32[]{:S(2)}) collective-permute-start(bf16[1152,1536]{1,0:T(8,128)(2,1)} %pad_maximum_fusion), channel_id=1, source_target_pairs={{0,1},{1,0},{2,3},{3,2},{4,5},{5,4},{6,7},{7,6},{8,9},{9,8},{10,11... | collective-permute-start | bytes 10616840 | tf_op jit(solution)/shard_map/ppermute | solution.py:367
  154.6 21.3 %collective-permute-start.11 = (bf16[144,2560]{1,0:T(8,128)(2,1)S(1)}, bf16[144,2560]{1,0:T(8,128)(2,1)S(1)}, u32[]{:S(2)}, u32[]{:S(2)}) collective-permute-start(bf16[144,2560]{1,0:T(8,128)(2,1)S(1)} %get-tuple-element.42), channel_id=1, source_target_pairs={{0,2},{2,0},{1,3},{3,1},{16,18},{18,16},{17,19},{19,17}} | collective-permute-start | bytes 2211848 | tf_op jit(solution)/shard_map/ppermute | solution.py:299
  162.8 42.7 %collective-permute-start.24 = (bf16[256,1280]{1,0:T(8,128)(2,1)}, bf16[256,1280]{1,0:T(8,128)(2,1)S(1)}, u32[]{:S(2)}, u32[]{:S(2)}) collective-permute-start(bf16[256,1280]{1,0:T(8,128)(2,1)} %collective-permute-done.3), channel_id=1, source_target_pairs={{0,2},{2,0},{4,6},{6,4},{1,3},{3,1},{5,7},{7,5},{16,18},{18,16},{2... | collective-permute-start | bytes 1966088 | tf_op jit(solution)/shard_map/ppermute | solution.py:273
  166.2 35.8 %collective-permute-start.10 = (bf16[144,2560]{1,0:T(8,128)(2,1)S(1)}, bf16[144,2560]{1,0:T(8,128)(2,1)S(1)}, u32[]{:S(2)}, u32[]{:S(2)}) collective-permute-start(bf16[144,2560]{1,0:T(8,128)(2,1)S(1)} %get-tuple-element.43), channel_id=1, source_target_pairs={{0,2},{2,0},{4,6},{6,4},{1,3},{3,1},{5,7},{7,5},{16,18},{18,16},{2... | collective-permute-start | bytes 2211848 | tf_op jit(solution)/shard_map/ppermute | solution.py:299
  176.1 28.4 %collective-permute-start.12 = (bf16[144,2560]{1,0:T(8,128)(2,1)S(1)}, bf16[144,2560]{1,0:T(8,128)(2,1)S(1)}, u32[]{:S(2)}, u32[]{:S(2)}) collective-permute-start(bf16[144,2560]{1,0:T(8,128)(2,1)S(1)} %fusion.34), channel_id=1, source_target_pairs={{0,4},{2,6},{1,5},{3,7},{16,20},{18,22},{17,21},{19,23}} | collective-permute-start | bytes 2211848 | tf_op jit(solution)/shard_map/ppermute | solution.py:308
  179.5 29.6 %collective-permute-start.25 = (bf16[256,1280]{1,0:T(8,128)(2,1)}, bf16[256,1280]{1,0:T(8,128)(2,1)S(1)}, u32[]{:S(2)}, u32[]{:S(2)}) collective-permute-start(bf16[256,1280]{1,0:T(8,128)(2,1)} %collective-permute-done.2), channel_id=1, source_target_pairs={{8,10},{10,8},{12,14},{14,12},{9,11},{11,9},{13,15},{15,13},{24,26... | collective-permute-start | bytes 1966088 | tf_op jit(solution)/shard_map/ppermute | solution.py:273
  202.1 16.7 %collective-permute-start.9 = (bf16[144,2560]{1,0:T(8,128)(2,1)S(1)}, bf16[144,2560]{1,0:T(8,128)(2,1)S(1)}, u32[]{:S(2)}, u32[]{:S(2)}) collective-permute-start(bf16[144,2560]{1,0:T(8,128)(2,1)S(1)} %get-tuple-element.44), channel_id=1, source_target_pairs={{0,2},{2,0},{4,6},{6,4},{8,10},{10,8},{1,3},{3,1},{5,7},{7,5},{9,1... | collective-permute-start | bytes 2211848 | tf_op jit(solution)/shard_map/ppermute | solution.py:299
  204.5 15.8 %collective-permute-start.17 = (bf16[144,2560]{1,0:T(8,128)(2,1)S(1)}, bf16[144,2560]{1,0:T(8,128)(2,1)S(1)}, u32[]{:S(2)}, u32[]{:S(2)}) collective-permute-start(bf16[144,2560]{1,0:T(8,128)(2,1)S(1)} %get-tuple-element.39), channel_id=1, source_target_pairs={{12,14},{14,12},{13,15},{15,13},{28,30},{30,28},{29,31},{31,29}} | collective-permute-start | bytes 2211848 | tf_op jit(solution)/shard_map/ppermute | solution.py:299
  205.5 17.2 %collective-permute-start.13 = (bf16[144,2560]{1,0:T(8,128)(2,1)S(1)}, bf16[144,2560]{1,0:T(8,128)(2,1)S(1)}, u32[]{:S(2)}, u32[]{:S(2)}) collective-permute-start(bf16[144,2560]{1,0:T(8,128)(2,1)S(1)} %fusion.36), channel_id=1, source_target_pairs={{0,4},{2,6},{4,8},{6,10},{1,5},{3,7},{5,9},{7,11},{16,20},{18,22},... | collective-permute-start | bytes 2211848 | tf_op jit(solution)/shard_map/ppermute | solution.py:308
  209.1 30.4 %collective-permute-start.16 = (bf16[144,2560]{1,0:T(8,128)(2,1)S(1)}, bf16[144,2560]{1,0:T(8,128)(2,1)S(1)}, u32[]{:S(2)}, u32[]{:S(2)}) collective-permute-start(bf16[144,2560]{1,0:T(8,128)(2,1)S(1)} %get-tuple-element.40), channel_id=1, source_target_pairs={{8,10},{10,8},{12,14},{14,12},{9,11},{11,9},{13,15},{15,13},{24,26... | collective-permute-start | bytes 2211848 | tf_op jit(solution)/shard_map/ppermute | solution.py:299
  218.8 48.5 %collective-permute-start.15 = (bf16[144,2560]{1,0:T(8,128)(2,1)}, bf16[144,2560]{1,0:T(8,128)(2,1)}, u32[]{:S(2)}, u32[]{:S(2)}) collective-permute-start(bf16[144,2560]{1,0:T(8,128)(2,1)} %get-tuple-element.41), channel_id=1, source_target_pairs={{4,6},{6,4},{8,10},{10,8},{12,14},{14,12},{5,7},{7,5},{9,11},{11,9... | collective-permute-start | bytes 2211848 | tf_op jit(solution)/shard_map/ppermute | solution.py:299
  220.3 16.6 %collective-permute-start.26 = (bf16[256,1280]{1,0:T(8,128)(2,1)S(1)}, bf16[256,1280]{1,0:T(8,128)(2,1)S(1)}, u32[]{:S(2)}, u32[]{:S(2)}) collective-permute-start(bf16[256,1280]{1,0:T(8,128)(2,1)S(1)} %collective-permute-done.5), channel_id=1, source_target_pairs={{0,2},{2,0},{1,3},{3,1},{16,18},{18,16},{17,19},{19,17}} | collective-permute-start | bytes 1966088 | tf_op jit(solution)/shard_map/ppermute | solution.py:273
  224.1 15.4 %collective-permute-start.18 = (bf16[144,2560]{1,0:T(8,128)(2,1)S(1)}, bf16[144,2560]{1,0:T(8,128)(2,1)S(1)}, u32[]{:S(2)}, u32[]{:S(2)}) collective-permute-start(bf16[144,2560]{1,0:T(8,128)(2,1)S(1)} %get-tuple-element.46), channel_id=1, source_target_pairs={{12,8},{14,10},{13,9},{15,11},{28,24},{30,26},{29,25},{31,27}} | collective-permute-start | bytes 2211848 | tf_op jit(solution)/shard_map/ppermute | solution.py:308
  236.9 38.0 %collective-permute-start.8 = (bf16[144,2560]{1,0:T(8,128)(2,1)}, bf16[144,2560]{1,0:T(8,128)(2,1)}, u32[]{:S(2)}, u32[]{:S(2)}) collective-permute-start(bf16[144,2560]{1,0:T(8,128)(2,1)} %get-tuple-element.38), channel_id=1, source_target_pairs={{0,2},{2,0},{4,6},{6,4},{8,10},{10,8},{12,14},{14,12},{1,3},{3,1},... | collective-permute-start | bytes 2211848 | tf_op jit(solution)/shard_map/ppermute | solution.py:299
  240.7 26.6 %collective-permute-start.19 = (bf16[144,2560]{1,0:T(8,128)(2,1)}, bf16[144,2560]{1,0:T(8,128)(2,1)}, u32[]{:S(2)}, u32[]{:S(2)}) collective-permute-start(bf16[144,2560]{1,0:T(8,128)(2,1)} %fusion.31), channel_id=1, source_target_pairs={{8,4},{10,6},{12,8},{14,10},{9,5},{11,7},{13,9},{15,11},{24,20},{2... | collective-permute-start | bytes 2211848 | tf_op jit(solution)/shard_map/ppermute | solution.py:308
  269.2 13.4 %collective-permute-start.20 = (bf16[144,2560]{1,0:T(8,128)(2,1)S(1)}, bf16[144,2560]{1,0:T(8,128)(2,1)S(1)}, u32[]{:S(2)}, u32[]{:S(2)}) collective-permute-start(bf16[144,2560]{1,0:T(8,128)(2,1)S(1)} %fusion.33), channel_id=1, source_target_pairs={{4,0},{6,2},{8,4},{10,6},{12,8},{14,10},{5,1},{7,3},{9,5},{11,7},{... | collective-permute-start | bytes 2211848 | tf_op jit(solution)/shard_map/ppermute | solution.py:308
  (24 other events, 349.0 us)

commit v3 on v1

--- a/solution.py
+++ b/solution.py
@@ -459,6 +459,23 @@
         + right_t(sh_gate, s_gate)
         + right_t(sh_up, s_up)
     ).astype(jnp.bfloat16)
+    hidden = mine.shape[1]
+
+    def to_tokens(one_hot, values):
+        return jnp.einsum(
+            "bst,bsf->btf", one_hot, values.reshape(blocks, CAP, hidden),
+            preferred_element_type=jnp.float32,
+        )
+
+    by_token = (
+        (to_tokens(to_slots, mine) + to_tokens(to_slots_b, other))
+        .astype(jnp.bfloat16)
+        .reshape(blocks * rows, hidden)
+    )
+    wide = hidden // 3
+    dy_half = lax.dynamic_slice_in_dim(dy_all.reshape(blocks * rows, width), node * half, half, 1)
+    grad_down = left_t(by_token[:, 2 * wide:], dy_half)
+    partial_in, by_token, grad_down = lax.optimization_barrier((partial_in, by_token, grad_down))
     returned = reduce_rows(partial_in.reshape(count // 2, 2, 2 * CAP, width), count)
 
     own_ids = expert_ids[:, 0].reshape(1, rows)
@@ -467,23 +484,6 @@
         (jnp.arange(2) == node)[None, :, None, None], picks[:, None], jnp.zeros((), jnp.bfloat16)
     ).reshape(4 * CAP, rows)
     grad_tokens = left_t(picks, returned.reshape(4 * CAP, width)).astype(jnp.bfloat16)
-
-    hidden = mine.shape[1]
-
-    def to_tokens(one_hot, values):
-        return jnp.einsum(
-            "bst,bsf->btf", one_hot, values.reshape(blocks, CAP, hidden),
-            preferred_element_type=jnp.float32,
-        )
-
-    by_token = (
-        (to_tokens(to_slots, mine) + to_tokens(to_slots_b, other))
-        .astype(jnp.bfloat16)
-        .reshape(blocks * rows, hidden)
-    )
-    wide = hidden // 3
-    dy_half = lax.dynamic_slice_in_dim(dy_all.reshape(blocks * rows, width), node * half, half, 1)
-    grad_down = left_t(by_token[:, 2 * wide:], dy_half)
     grad_gate = left_t(x_all, by_token[:, :wide])
     grad_up = left_t(x_all, by_token[:, wide:2 * wide])
     return (grad_tokens, grad_gate, grad_up, grad_down)

time: 255 us -> 248 us (0.973); the launches traced: 252 us -> 248 us
  Pallas kernels: 154 us -> 136 us
  matrix products: 78.1 us -> 92.4 us
    pallas_call x1, Pallas kernels: 89.1 us -> 71.6 us  [reduce_rows(): pl.pallas_call(functools.partial(reduce_kernel, depth), out_shape=jax.Sha...]
    dot_general x6, matrix products: 37.1 us -> 46.7 us  [right_t(): lax.dot_general(left, right, (((1,), (1,)), ((), ())), preferred_element_...]
    dot_general x2, matrix products: 10.5 us -> 15.2 us  [to_tokens(): jnp.einsum('bst,bsf->btf', one_hot, values.reshape(blocks, CAP, hidden),...]
  transfers between devices with their start and end apart: 2 -> 2, of which waited for: 0 -> 0; matrix products, arithmetic and copies ran while one was open for 27% -> 33% of each run, Pallas kernels for 35% -> 29%
where the time goes in v3:
time: 248 us
  Pallas kernels  136 us (55%)
  matrix products  92.4 us (37%)
  between operations  14.2 us (6%)
  other arithmetic  3.34 us (1%)
    pallas_call x1, Pallas kernels, reduce_rows(): pl.pallas_call(functools.partial(reduce_kernel, depth), out_shape=jax.Sha...  71.6 us
    pallas_call x1, Pallas kernels, gather(): pl.pallas_call(functools.partial(gather_kernel, depth), out_shape=(jax.Sh...  64.5 us
    dot_general x6, matrix products, right_t(): lax.dot_general(left, right, (((1,), (1,)), ((), ())), preferred_element_...  46.7 us
    dot_general x4, matrix products, left_t(): lax.dot_general(left, right, (((0,), (0,)), ((), ())), preferred_element_...  24.2 us
    dot_general x2, matrix products, to_tokens(): jnp.einsum('bst,bsf->btf', one_hot, values.reshape(blocks, CAP, hidden),...  15.2 us
    dot_general x1, matrix products, body(): jnp.einsum('bst,btd->bsd', to_slots, dy_all, preferred_element_type=jnp.f...  5.81 us
  transfers between devices with their start and end apart: 2, of which 0 were waited for; matrix products, arithmetic and copies ran while one was open for 33% of the time, Pallas kernels for 29%

profile of v3, /device:TPU:0, one launch (start us, length us, event | category | flops | bytes accessed | tf_op | source)
XLA Modules:
  0.0 248.2 jit_solution(17632807008523867223)
XLA Ops:
  7.2 1.4 broadcast_in_dim.24.ids
  8.6 64.5 %gather_rows.1 = (bf16[8,2,128,2560]{3,2,1,0:T(8,128)(2,1)}, s32[8,2,8,128]{3,2,1,0:T(8,128)}, bf16[2,128,1280]{2,1,0:T(8,128)(2,1)}) custom-call(bf16[128,2560]{1,0:T(8,128)(2,1)} %dy.1, s32[8,128]{1,0:T(8,128)} %broadcast_in_dim.24.ids, bf16[128,2560]{1,0:T(8,128)(2,1)} %x.1), custom_call_target="tpu_custom_call" | custom-call | tf_op jit(solution)/shard_map/gather_rows/pallas_call | solution.py:209
  73.1 0.9 compare_reduce_fusion
  74.1 0.1 fusion.41
  74.2 5.8 %convolution_convert_fusion = bf16[16,72,2560]{2,1,0:T(8,128)(2,1)S(1)} fusion(bf16[16,128,2560]{2,1,0:T(8,128)(2,1)} %bitcast.96, s32[16,128]{1,0:T(8,128)S(1)} %fusion.41), kind=kOutput, calls=%fused_computation.5 | convolution fusion | flops 758071296 | bytes 16392192 | tf_op jit(solution)/shard_map/bst,btd->bsd/dot_general | solution.py:435
  80.0 4.3 %multiply_convert_fusion = (bf16[1152,512]{1,0:T(8,128)(2,1)S(1)}, bf16[1152,512]{1,0:T(8,128)(2,1)S(1)}, bf16[1152,512]{1,0:T(8,128)(2,1)S(1)}) fusion(bf16[2,1152,512]{2,1,0:T(8,128)(2,1)S(1)} %copy-done.11, bf16[1152,2560]{1,0:T(8,128)(2,1)S(1)} %bitcast.98, bf16[512,2560]{1,0:T(8,128)(2,1)S(1)} %copy-done.9), kind=kOutput, calls=%fused_computation.41 | convolution fusion | flops 3029925888 | bytes 14417920 | tf_op jit(solution)/shard_map/dot_general | solution.py:25
  84.4 2.3 pad_maximum_fusion
  86.7 0.2 copy-done.6
  86.9 0.4 collective-permute-start
  87.4 0.1 fusion.47
  87.5 0.1 fusion.44
  87.8 8.6 %fusion.50 = f32[16,128,1536]{2,1,0:T(8,128)} fusion(bf16[16,72,1536]{2,1,0:T(8,128)(2,1)} %bitcast.18, s32[16,128]{1,0:T(8,128)S(1)} %fusion.41), kind=kOutput, calls=%fused_computation.71 | convolution fusion | flops 453132288 | bytes 16130048 | tf_op jit(solution)/shard_map/bst,bsf->btf/dot_general | solution.py:465
  96.3 5.5 %fusion.6 = f32[1152,512]{1,0:T(8,128)S(1)} fusion(bf16[1152,2560]{1,0:T(8,128)(2,1)} %bitcast.99, bf16[1,512,2560]{2,1,0:T(8,128)(2,1)S(1)} %copy-done.10), kind=kOutput, calls=%fused_computation.21 | convolution fusion | flops 3019898880 | bytes 10878976 | tf_op jit(solution)/shard_map/dot_general | solution.py:25
  101.8 7.5 %fusion.4 = f32[1152,2560]{1,0:T(8,128)} fusion(bf16[1,2560,512]{2,1,0:T(8,128)(2,1)S(1)} %copy-done, f32[1152,512]{1,0:T(8,128)S(1)} %fusion.6, bf16[2,1152,512]{2,1,0:T(8,128)(2,1)S(1)} %copy-done.5), kind=kOutput, calls=%fused_computation.19 | convolution fusion | flops 3026976768 | bytes 19136512 | tf_op jit(solution)/shard_map/dot_general | solution.py:25
  109.3 0.1 fusion.39
  109.5 8.2 %convolution_add_fusion.2 = f32[1152,2560]{1,0:T(8,128)S(1)} fusion(f32[1152,2560]{1,0:T(8,128)} %fusion.4, bf16[1,2560,512]{2,1,0:T(8,128)(2,1)S(1)} %copy-done.4, f32[1152,512]{1,0:T(8,128)S(1)} %fusion.6, bf16[2,1152,512]{2,1,0:T(8,128)(2,1)} %param.14), kind=kOutput, calls=%fused_computation.2 | convolution fusion | flops 3026976768 | bytes 29753344 | tf_op jit(solution)/shard_map/dot_general | solution.py:25
  117.7 9.8 %convolution_add_fusion.1 = f32[1152,2560]{1,0:T(8,128)} fusion(f32[1152,2560]{1,0:T(8,128)S(1)} %convolution_add_fusion.2, bf16[1152,512]{1,0:T(8,128)(2,1)} %copy-done.3, bf16[2560,512]{1,0:T(8,128)(2,1)} %param.19), kind=kOutput, calls=%fused_computation.1 | convolution fusion | flops 3022848000 | bytes 27394048 | tf_op jit(solution)/shard_map/dot_general | solution.py:25
  127.5 11.4 %fusion = bf16[1152,2560]{1,0:T(8,128)(2,1)} fusion(f32[1152,2560]{1,0:T(8,128)} %convolution_add_fusion.1, bf16[1152,512]{1,0:T(8,128)(2,1)} %copy-done.6, bf16[2560,512]{1,0:T(8,128)(2,1)} %param.20), kind=kOutput, calls=%fused_computation.4 | convolution fusion | flops 3025797120 | bytes 21495808 | tf_op jit(solution)/shard_map/dot_general | solution.py:25
  138.9 6.7 %add_convert_fusion = bf16[16,128,1536]{2,1,0:T(8,128)(2,1)} fusion(f32[16,128,1536]{2,1,0:T(8,128)S(1)} %bitcast.95, bf16[16,72,1536]{2,1,0:T(8,128)(2,1)} %bitcast.19, s32[16,128]{1,0:T(8,128)S(1)} %fusion.39), kind=kOutput, calls=%fused_computation.3 | convolution fusion | flops 459423744 | bytes 22421504 | tf_op jit(solution)/shard_map/bst,bsf->btf/dot_general | solution.py:465
  145.6 7.6 %fusion.1 = f32[512,1280]{1,0:T(8,128)} fusion(bf16[2048,2560]{1,0:T(8,128)(2,1)} %bitcast.97, s32[]{:T(128)S(6)} %select_n.39, bf16[2048,1536]{1,0:T(8,128)(2,1)} %bitcast.100), kind=kOutput, calls=%fused_computation.6 | convolution fusion | flops 2684354560 | bytes 9961476 | tf_op jit(solution)/shard_map/dot_general | solution.py:31
  153.2 71.6 %reduce_rows.1 = bf16[2,144,2560]{2,1,0:T(8,128)(2,1)} custom-call(bf16[4,2,144,2560]{3,2,1,0:T(8,128)(2,1)} %bitcast.103), custom_call_target="tpu_custom_call" | custom-call | tf_op jit(solution)/shard_map/reduce_rows/pallas_call | solution.py:388
  224.7 2.7 %convolution_convert_fusion.1 = bf16[128,2560]{1,0:T(8,128)(2,1)} fusion(bf16[288,128]{1,0:T(8,128)(2,1)S(1)} %bitcast.106, bf16[288,2560]{1,0:T(8,128)(2,1)} %bitcast.104), kind=kOutput, calls=%fused_computation.8 | convolution fusion | flops 189071360 | bytes 2203648 | tf_op jit(solution)/shard_map/dot_general | solution.py:31
  227.5 7.7 %fusion.28 = f32[1280,512]{1,0:T(8,128)} fusion(bf16[2048,1280]{1,0:T(8,128)(2,1)} %all-gather.2.cloned.1.call-done, bf16[2048,1536]{1,0:T(8,128)(2,1)} %bitcast.101), kind=kOutput, calls=%fused_computation.45 | convolution fusion | flops 2684354560 | bytes 9961472 | tf_op jit(solution)/shard_map/dot_general | solution.py:31
  235.2 6.2 %fusion.26 = f32[1280,512]{1,0:T(8,128)} fusion(bf16[2048,1280]{1,0:T(8,128)(2,1)S(1)} %copy-done.8, bf16[2048,1536]{1,0:T(8,128)(2,1)} %bitcast.102), kind=kOutput, calls=%fused_computation.43 | convolution fusion | flops 2684354560 | bytes 9961472 | tf_op jit(solution)/shard_map/dot_general | solution.py:31
  (40 shorter events, 0.3 us)
Async XLA Ops:
  7.2 94.6 %copy-start = (bf16[1,2560,512]{2,1,0:T(8,128)(2,1)S(1)}, bf16[1,2560,512]{2,1,0:T(8,128)(2,1)}, u32[]{:S(2)}) copy-start(bf16[1,2560,512]{2,1,0:T(8,128)(2,1)} %param.16) | copy-start | bytes 7864324
  7.2 220.3 %all-gather.2.cloned.1.call-start = ((), (), s32[]{:S(2)}) async-start(), calls=%async_computation | async-start | bytes 5898240 | tf_op jit(solution)/shard_map/all_gather | solution.py:428
  74.2 5.8 %copy-start.9 = (bf16[512,2560]{1,0:T(8,128)(2,1)S(1)}, bf16[512,2560]{1,0:T(8,128)(2,1)}, u32[]{:S(2)}) copy-start(bf16[512,2560]{1,0:T(8,128)(2,1)} %param.21) | copy-start | bytes 7864324
  74.2 5.8 %copy-start.11 = (bf16[2,1152,512]{2,1,0:T(8,128)(2,1)S(1)}, bf16[2,1152,512]{2,1,0:T(8,128)(2,1)}, u32[]{:S(2)}) copy-start(bf16[2,1152,512]{2,1,0:T(8,128)(2,1)} %param.15) | copy-start | bytes 7077892
  80.0 4.4 %copy-start.2 = (bf16[16,72,2560]{2,1,0:T(8,128)(2,1)}, bf16[16,72,2560]{2,1,0:T(8,128)(2,1)S(1)}, u32[]{:S(2)}) copy-start(bf16[16,72,2560]{2,1,0:T(8,128)(2,1)S(1)} %convolution_convert_fusion) | copy-start | bytes 17694724
  84.4 2.4 copy-start.3
  84.4 2.6 %copy-start.6 = (bf16[1152,512]{1,0:T(8,128)(2,1)}, bf16[1152,512]{1,0:T(8,128)(2,1)S(1)}, u32[]{:S(2)}) copy-start(bf16[1152,512]{1,0:T(8,128)(2,1)S(1)} %get-tuple-element.18) | copy-start | bytes 3538948
  84.4 3.0 %copy-start.7 = (s32[128,1]{0,1:T(1,128)S(1)}, s32[128,1]{0,1:T(1,128)}, u32[]{:S(2)}) copy-start(s32[128,1]{0,1:T(1,128)} %param.13) | copy-start | bytes 1540
  86.9 52.0 %collective-permute-start = (bf16[1152,1536]{1,0:T(8,128)(2,1)}, bf16[1152,1536]{1,0:T(8,128)(2,1)}, u32[]{:S(2)}, u32[]{:S(2)}) collective-permute-start(bf16[1152,1536]{1,0:T(8,128)(2,1)} %pad_maximum_fusion), channel_id=1, source_target_pairs={{0,1},{1,0},{2,3},{3,2},{4,5},{5,4},{6,7},{7,6},{8,9},{9,8},{10,11... | collective-permute-start | bytes 10616840 | tf_op jit(solution)/shard_map/ppermute | solution.py:448
  87.8 8.6 %copy-start.10 = (bf16[1,512,2560]{2,1,0:T(8,128)(2,1)S(1)}, bf16[1,512,2560]{2,1,0:T(8,128)(2,1)}, u32[]{:S(2)}) copy-start(bf16[1,512,2560]{2,1,0:T(8,128)(2,1)} %param.18) | copy-start | bytes 7864324
  96.3 5.5 %copy-start.5 = (bf16[2,1152,512]{2,1,0:T(8,128)(2,1)S(1)}, bf16[2,1152,512]{2,1,0:T(8,128)(2,1)}, u32[]{:S(2)}) copy-start(bf16[2,1152,512]{2,1,0:T(8,128)(2,1)} %param.14) | copy-start | bytes 7077892
  101.8 7.7 %copy-start.4 = (bf16[1,2560,512]{2,1,0:T(8,128)(2,1)S(1)}, bf16[1,2560,512]{2,1,0:T(8,128)(2,1)}, u32[]{:S(2)}) copy-start(bf16[1,2560,512]{2,1,0:T(8,128)(2,1)} %param.17) | copy-start | bytes 7864324
  117.6 21.3 %slice-start = ((s8[12582912]{0:T(1024)(128)(4,1)}), s8[4194304]{0:T(1024)(128)(4,1)S(1)}, s32[]{:S(2)}) async-start(s8[12582912]{0:T(1024)(128)(4,1)} %bitcast.94), calls=%async_computation.1 | async-start | bytes 8388608
  117.7 21.3 %slice-start.1 = ((s8[12582912]{0:T(1024)(128)(4,1)}), s8[4194304]{0:T(1024)(128)(4,1)S(1)}, s32[]{:S(2)}) async-start(s8[12582912]{0:T(1024)(128)(4,1)} %bitcast.94), calls=%async_computation.2 | async-start | bytes 8388608
  127.5 11.4 %slice-start.2 = ((s8[12582912]{0:T(1024)(128)(4,1)}), s8[4194304]{0:T(1024)(128)(4,1)S(1)}, s32[]{:S(2)}) async-start(s8[12582912]{0:T(1024)(128)(4,1)} %bitcast.94), calls=%async_computation.3 | async-start | bytes 8388608
  227.5 7.7 %copy-start.8 = (bf16[2048,1280]{1,0:T(8,128)(2,1)S(1)}, bf16[2048,1280]{1,0:T(8,128)(2,1)}, u32[]{:S(2)}) copy-start(bf16[2048,1280]{1,0:T(8,128)(2,1)} %all-gather.2.cloned.1.call-done) | copy-start | bytes 15728644
  235.2 6.2 %copy-start.1 = (bf16[1,2560,512]{2,1,0:T(8,128)(2,1)S(1)}, bf16[1,2560,512]{2,1,0:T(8,128)(2,1)}, u32[]{:S(2)}) copy-start(bf16[1,2560,512]{2,1,0:T(8,128)(2,1)} %param.16) | copy-start | bytes 7864324
Sparse Core Ops, SparseCore 0:
  73.3 86.4 all-gather.1
